TPU v7x, 32 devices: a whole 2x2x4 slice. The times are simulated.
32 devices in a mesh: rep: 8 (over z, x), tp: 4 (over y, core).
Axes of the slice: x: 2, y: 2, z: 4, core: 2. Of those that a mesh axis runs over, the one named last changes fastest.
Arguments:
- queries: bfloat16 [8, 512, 1024], P('rep', None, 'tp'), may hold values from -120 to 120
- keys: bfloat16 [8, 512, 1024], P('rep', None, 'tp'), may hold values from -6 to 6
- values: bfloat16 [8, 512, 1024], P('rep', None, 'tp'), may hold values from -6 to 6
- out_weight: bfloat16 [8, 1024, 7168], P('rep', 'tp'), may hold values from -0.1875 to 0.1875
- cotangent: bfloat16 [8, 512, 7168], P('rep', 'tp'), may hold values from -6 to 6
- local_params: bfloat16 [8, 2, 32, 7168], P('rep', None, 'tp'), may hold values from -6 to 6
- global_params: float32 [2, 32, 7168], P(None, 'tp'), may hold values from -6 to 6
- momentum: float32 [2, 32, 7168], P(None, 'tp'), may hold values from -3 to 3
- frag_index: int32 [1], replicated, may hold values from 0 to 1
Outputs:
- branch_out: bfloat16 [8, 512, 7168], P('rep', 'tp')
- weight_grad: bfloat16 [8, 1024, 7168], P('rep', 'tp')
- query_grad: bfloat16 [8, 512, 1024], P('rep', None, 'tp')
- key_grad: bfloat16 [8, 512, 1024], P('rep', None, 'tp')
- value_grad: bfloat16 [8, 512, 1024], P('rep', None, 'tp')
- new_global: float32 [32, 7168], P('tp')
- new_momentum: float32 [32, 7168], P('tp')
All inputs are finite; a program needn't handle non-finite values.
Results may differ from a plain program's by a relative error of at most 0.017.
Values may be sent and summed in bfloat16 or wider, within the bound.
A program may use at most 128 MiB of HBM per device.

v0:
```python
import jax
import jax.numpy as jnp
from jax import lax
from jax.sharding import PartitionSpec as P

HD = 128
LEN = 512
SEQS = 1


outer_momentum = 0.9
outer_rate = 0.7


def nesterov(outer_old, moment_old, summed):
    average = summed / lax.axis_size("rep")
    pseudo_grad = outer_old - average
    new_momentum = outer_momentum * moment_old + pseudo_grad
    new_global = outer_old - outer_rate * (outer_momentum * new_momentum + pseudo_grad)
    return (new_global, new_momentum)


def outer_update(local_params, global_params, momentum, frag_index):
    chosen = frag_index[0]
    local_sel = lax.dynamic_index_in_dim(local_params[0], chosen, 0, keepdims=False).astype(
        jnp.float32
    )
    outer_old = lax.dynamic_index_in_dim(global_params, chosen, 0, keepdims=False)
    moment_old = lax.dynamic_index_in_dim(momentum, chosen, 0, keepdims=False)
    summed = lax.psum(local_sel.astype(jnp.bfloat16), "rep").astype(jnp.float32)
    return nesterov(outer_old, moment_old, summed)


def inner_step(queries, keys, values, out_weight, cotangent):
    scale = HD ** (-0.5)
    head_cols = queries.shape[2]
    heads_here = head_cols // HD
    tokens = queries.shape[1]
    weight_here = out_weight[0]
    query_heads = queries[0].reshape(SEQS, LEN, heads_here, HD)
    key_heads = keys[0].reshape(SEQS, LEN, heads_here, HD)
    value_heads = values[0].reshape(SEQS, LEN, heads_here, HD)
    scores = (
        jnp.einsum("slhd,smhd->shlm", query_heads, key_heads, preferred_element_type=jnp.float32)
        * scale
    )
    causal = jnp.arange(LEN)[:, None] >= jnp.arange(LEN)[None, :]
    scores = jnp.where(causal[None, None], scores, -1e30)
    top = jnp.max(scores, axis=-1, keepdims=True)
    weights = jnp.exp(scores - top)
    probs = weights / jnp.sum(weights, axis=-1, keepdims=True)
    probs_half = probs.astype(jnp.bfloat16)
    context = jnp.einsum(
        "shlm,smhd->slhd", probs_half, value_heads, preferred_element_type=jnp.float32
    )
    context = context.astype(jnp.bfloat16).reshape(tokens, head_cols)
    context_rows = context
    branch_out = lax.psum_scatter(
        jnp.dot(context_rows, weight_here, preferred_element_type=jnp.float32).astype(jnp.bfloat16),
        "tp",
        scatter_dimension=0,
        tiled=True,
    )
    block_rows = lax.all_gather(cotangent[0], "tp", axis=0, tiled=True)
    part_grad = lax.dot_general(
        block_rows, weight_here, (((1,), (1,)), ((), ())), preferred_element_type=jnp.float32
    )
    context_acc = part_grad
    context_rows = context
    weight_acc = lax.dot_general(
        context_rows, block_rows, (((0,), (0,)), ((), ())), preferred_element_type=jnp.float32
    )
    context_acc, weight_acc = (context_acc, weight_acc)
    weight_grad = weight_acc.astype(jnp.bfloat16)
    context_grad = context_acc.astype(jnp.bfloat16).reshape(SEQS, LEN, heads_here, HD)
    probs_grad = jnp.einsum(
        "slhd,smhd->shlm", context_grad, value_heads, preferred_element_type=jnp.float32
    )
    inner = jnp.sum(probs * probs_grad, axis=-1, keepdims=True)
    score_grad = (probs * (probs_grad - inner) * scale).astype(jnp.bfloat16)
    query_grad = jnp.einsum(
        "shlm,smhd->slhd", score_grad, key_heads, preferred_element_type=jnp.float32
    )
    key_grad = jnp.einsum(
        "shlm,slhd->smhd", score_grad, query_heads, preferred_element_type=jnp.float32
    )
    value_grad = jnp.einsum(
        "shlm,slhd->smhd", probs_half, context_grad, preferred_element_type=jnp.float32
    )
    shaped = [
        g.astype(jnp.bfloat16).reshape(1, tokens, head_cols)
        for g in (query_grad, key_grad, value_grad)
    ]
    return (branch_out[None], weight_grad[None], shaped[0], shaped[1], shaped[2])


def shards(
    queries, keys, values, out_weight, cotangent, local_params, global_params, momentum, frag_index
):
    results = inner_step(queries, keys, values, out_weight, cotangent)
    new_global, new_momentum = outer_update(local_params, global_params, momentum, frag_index)
    return (results[0], results[1], results[2], results[3], results[4], new_global, new_momentum)


def solution(mesh):
    placed = (
        P("rep", None, "tp"),
        P("rep", None, "tp"),
        P("rep", None, "tp"),
        P("rep", "tp", None),
        P("rep", "tp", None),
        P("rep", None, "tp", None),
        P(None, "tp", None),
        P(None, "tp", None),
        P(),
    )
    return jax.shard_map(
        shards,
        mesh=mesh,
        in_specs=placed,
        out_specs=(
            P("rep", "tp", None),
            P("rep", "tp", None),
            P("rep", None, "tp"),
            P("rep", None, "tp"),
            P("rep", None, "tp"),
            P("tp", None),
            P("tp", None),
        ),
        check_vma=False,
    )
```

profile of v0, /device:TPU:0, one launch (start us, length us, event | category | flops | bytes accessed | tf_op | source)
XLA Modules:
  0.0 142.3 jit_solution(3032736122136269171)
XLA Ops:
  8.0 0.0 copy-start
  8.0 0.0 copy-start.1
  8.0 0.0 copy-start.2
  8.0 0.0 copy-start.3
  8.0 0.0 all-reduce.2.cloned.1.call-start
  8.8 0.1 copy-done
  8.9 0.7 dynamic-slice_bitcast_fusion
  9.6 0.0 all-reduce.2.cloned.1.call-update
  9.6 0.0 all-gather.3.cloned.1.call-start
  9.7 0.5 all-gather.3.cloned.1.call-update
  10.2 0.0 reduce-scatter.2.cloned.1.call-start
  10.3 0.0 copy-done.1
  10.3 0.1 copy.35
  10.4 0.0 copy-done.2
  10.4 0.1 copy.36
  10.6 0.0 copy-done.3
  10.6 0.0 copy-start.4
  10.6 0.1 reshape.115
  10.7 0.1 iota_compare_fusion
  10.7 0.0 copy-start.5
  10.8 2.3 %fusion.47 = (f32[2,512]{1,0:T(2,128)S(1)}, f32[2,512,512]{1,2,0:T(8,128)}) fusion(pred[512,512]{0,1:T(8,128)(4,1)S(1)} %iota_compare_fusion, bf16[512,2,128]{0,2,1:T(8,128)(2,1)S(1)} %bitcast.79, bf16[512,2,128]{0,2,1:T(8,128)(2,1)S(1)} %bitcast.83), kind=kOutput, calls=%fused_computation.46 | convolution fusion | flops 136315392 | bytes 2887680 | tf_op jit(solution)/shard_map/sub | solution.py:50
  13.1 0.0 copy-done.4
  13.1 0.0 copy-done.5
  13.1 1.3 convolution_convert_fusion.2
  14.4 7.4 %convolution_convert_fusion = bf16[512,7168]{1,0:T(8,128)(2,1)} fusion(bf16[512,256]{0,1:T(8,128)(2,1)S(1)} %bitcast.75, bf16[1,256,7168]{2,1,0:T(8,128)(2,1)} %param.12), kind=kOutput, calls=%fused_computation.2 | convolution fusion | flops 1882718208 | bytes 11272192 | tf_op jit(solution)/shard_map/dot_general | solution.py:59
  21.8 0.0 copy-start.6
  21.8 0.0 copy-start.7
  21.8 0.0 reduce-scatter.2.cloned.1.call-update
  21.8 63.3 %all-reduce.2.cloned.1.call-done = bf16[8,7168]{1,0:T(8,128)(2,1)} async-done(((bf16[8,7168]{1,0:T(8,128)(2,1)}), bf16[8,7168]{1,0:T(8,128)(2,1)}) %all-reduce.2.cloned.1.call-update) | async-done | bytes 114704 | tf_op jit(solution)/shard_map/psum | solution.py:30
  85.0 0.0 copy-done.6
  85.0 0.0 copy-done.7
  85.0 1.7 %bitcast_subtract_fusion = (f32[8,7168]{1,0:T(8,128)}, f32[8,7168]{1,0:T(8,128)}) fusion(bf16[8,7168]{1,0:T(8,128)(2,1)} %all-reduce.2.cloned.1.call-done, f32[2,8,7168]{2,1,0:T(8,128)S(1)} %copy-done.6, s32[]{:T(128)S(6)} %select_n.13, f32[2,8,7168]{2,1,0:T(8,128)S(1)} %copy-done.7), kind=kLoop, calls=%fused_computation.36 | loop fusion | flops 516096 | bytes 1032196 | tf_op jit(solution)/shard_map/sub | solution.py:19
  86.8 0.0 all-gather.3.cloned.1.call-done
  86.8 6.2 %fusion.24 = bf16[512,256]{0,1:T(8,128)(2,1)S(1)} fusion(bf16[1,256,7168]{2,1,0:T(8,128)(2,1)} %param.12, bf16[1,512,7168]{2,1,0:T(8,128)(2,1)} %all-gather.3.cloned.1.call-done), kind=kOutput, calls=%fused_computation.20 | convolution fusion | flops 1879179264 | bytes 11272192 | tf_op jit(solution)/shard_map/dot_general | solution.py:65
  93.0 0.4 fusion.37
  93.4 3.3 %fusion.18 = bf16[2,512,128]{1,2,0:T(8,128)(2,1)S(1)} fusion(bf16[512,2,128]{0,2,1:T(8,128)(2,1)} %bitcast.85, f32[2,512,512]{1,2,0:T(8,128)S(1)} %fusion.37, f32[2,512,512]{1,2,0:T(8,128)} %get-tuple-element.17, f32[2,512]{1,0:T(2,128)S(1)} %get-tuple-element.16), kind=kOutput, calls=%fused_computation.18 | convolution fusion | flops 138020352 | bytes 4722688 | tf_op jit(solution)/shard_map/shlm,smhd->slhd/dot_general | solution.py:81
  96.7 0.8 copy.27
  97.6 3.1 %fusion.21 = bf16[2,512,128]{1,2,0:T(8,128)(2,1)S(1)} fusion(bf16[512,2,128]{0,2,1:T(8,128)(2,1)S(1)} %bitcast.81, f32[2,512,512]{1,2,0:T(8,128)S(1)} %fusion.37, f32[2,512,512]{1,2,0:T(8,128)} %get-tuple-element.17, f32[2,512]{1,0:T(2,128)S(1)} %get-tuple-element.16), kind=kOutput, calls=%fused_computation.19 | convolution fusion | flops 138020352 | bytes 4722688 | tf_op jit(solution)/shard_map/shlm,slhd->smhd/dot_general | solution.py:84
  100.7 0.8 copy.28
  101.5 2.4 %convolution_convert_fusion.3 = bf16[2,128,512]{2,1,0:T(8,128)(2,1)S(1)} fusion(bf16[512,2,128]{0,2,1:T(8,128)(2,1)S(1)} %bitcast.78, f32[2,512]{1,0:T(2,128)S(1)} %get-tuple-element.16, pred[512,512]{0,1:T(8,128)(4,1)} %copy-done.5, bf16[512,2,128]{0,2,1:T(8,128)(2,1)S(1)} %bitcast.82, bf16[512,2,128]{0,2,1:T(8,128)(2,1)} %bitcast.86), kind=kOutput, calls=%fused_computation.22 | convolution fusion | flops 271189504 | bytes 1314816 | tf_op jit(solution)/shard_map/shlm,slhd->smhd/dot_general | solution.py:87
  103.9 0.8 copy.29
  104.7 7.1 %fusion.2 = bf16[1,256,7168]{2,1,0:T(8,128)(2,1)} fusion(bf16[512,256]{0,1:T(8,128)(2,1)S(1)} %bitcast.76, bf16[1,512,7168]{2,1,0:T(8,128)(2,1)} %all-gather.3.cloned.1.call-done), kind=kOutput, calls=%fused_computation.4 | convolution fusion | flops 1880883200 | bytes 11272192 | tf_op jit(solution)/shard_map/dot_general | solution.py:70
  111.9 23.0 %reduce-scatter.2.cloned.1.call-done = bf16[128,7168]{1,0:T(8,128)(2,1)} async-done(((bf16[512,7168]{1,0:T(8,128)(2,1)}), bf16[128,7168]{1,0:T(8,128)(2,1)}) %reduce-scatter.2.cloned.1.call-update) | async-done | bytes 1835024 | tf_op jit(solution)/shard_map/reduce_scatter | solution.py:58
Async XLA Ops:
  8.0 0.9 copy-start
  8.0 2.2 %copy-start.1 = (bf16[1,512,256]{2,1,0:T(8,128)(2,1)S(1)}, bf16[1,512,256]{2,1,0:T(8,128)(2,1)}, u32[]{:S(2)}) copy-start(bf16[1,512,256]{2,1,0:T(8,128)(2,1)} %param.9) | copy-start | bytes 786436
  8.0 2.4 %copy-start.2 = (bf16[1,512,256]{2,1,0:T(8,128)(2,1)S(1)}, bf16[1,512,256]{2,1,0:T(8,128)(2,1)}, u32[]{:S(2)}) copy-start(bf16[1,512,256]{2,1,0:T(8,128)(2,1)} %param.10) | copy-start | bytes 786436
  8.0 2.5 %copy-start.3 = (bf16[1,512,256]{2,1,0:T(8,128)(2,1)S(1)}, bf16[1,512,256]{2,1,0:T(8,128)(2,1)}, u32[]{:S(2)}) copy-start(bf16[1,512,256]{2,1,0:T(8,128)(2,1)} %param.11) | copy-start | bytes 786436
  8.0 77.0 %all-reduce.2.cloned.1.call-start = ((), (), s32[]{:S(2)}) async-start(), calls=%async_computation.2 | async-start | bytes 229376 | tf_op jit(solution)/shard_map/psum | solution.py:30
  9.6 77.2 %all-gather.3.cloned.1.call-start = ((), (), s32[]{:S(2)}) async-start(), calls=%async_computation.3 | async-start | bytes 9175040 | tf_op jit(solution)/shard_map/all_gather | solution.py:64
  10.2 124.7 %reduce-scatter.2.cloned.1.call-start = ((), (), s32[]{:S(2)}) async-start(), calls=%async_computation.1 | async-start | bytes 9175040 | tf_op jit(solution)/shard_map/reduce_scatter | solution.py:58
  10.6 2.5 %copy-start.4 = (bf16[1,512,256]{1,2,0:T(8,128)(2,1)}, bf16[1,512,256]{1,2,0:T(8,128)(2,1)S(1)}, u32[]{:S(2)}) copy-start(bf16[1,512,256]{1,2,0:T(8,128)(2,1)S(1)} %copy.36) | copy-start | bytes 786436
  10.7 2.3 %copy-start.5 = (pred[512,512]{0,1:T(8,128)(4,1)}, pred[512,512]{0,1:T(8,128)(4,1)S(1)}, u32[]{:S(2)}) copy-start(pred[512,512]{0,1:T(8,128)(4,1)S(1)} %iota_compare_fusion) | copy-start | bytes 786436
  21.8 63.3 %copy-start.6 = (f32[2,8,7168]{2,1,0:T(8,128)S(1)}, f32[2,8,7168]{2,1,0:T(8,128)}, u32[]{:S(2)}) copy-start(f32[2,8,7168]{2,1,0:T(8,128)} %param.15) | copy-start | bytes 1376260
  21.8 63.3 %copy-start.7 = (f32[2,8,7168]{2,1,0:T(8,128)S(1)}, f32[2,8,7168]{2,1,0:T(8,128)}, u32[]{:S(2)}) copy-start(f32[2,8,7168]{2,1,0:T(8,128)} %param.16) | copy-start | bytes 1376260
Sparse Core Ops, SparseCore 0:
  13.2 71.8 all-reduce.1
Sparse Core Ops, SparseCore 1:
  11.7 54.8 all-gather.2
  69.5 65.3 reduce-scatter.1
where the time goes:
time: 143 us; the launch traced here: 142 us
  waiting for transfers between devices  86.8 us (61%)
  matrix products  33.5 us (23%)
  between operations  16.4 us (11%)
  local copies, waits for them, and re-layouts  3.69 us (3%)
  other arithmetic  1.81 us (1%)
    psum x1, waiting for transfers between devices, outer_update(): summed = lax.psum(local_sel.astype(jnp.bfloat16), 'rep').astype(jnp.float32)  63.3 us
    reduce_scatter x1, waiting for transfers between devices, inner_step(): lax.psum_scatter(jnp.dot(context_rows, weight_here, preferred_element_typ...  23 us
    dot_general x1, matrix products, inner_step(): jnp.dot(context_rows, weight_here, preferred_element_type=jnp.float32)  7.37 us
    dot_general x1, matrix products, inner_step(): lax.dot_general(context_rows, block_rows, (((0,), (0,)), ((), ())), prefe...  7.12 us
    dot_general x1, matrix products, inner_step(): lax.dot_general(block_rows, weight_here, (((1,), (1,)), ((), ())), prefer...  6.21 us
    dot_general x1, matrix products, inner_step(): jnp.einsum('shlm,smhd->slhd', score_grad, key_heads, preferred_element_ty...  3.32 us
    dot_general x1, matrix products, inner_step(): jnp.einsum('shlm,slhd->smhd', score_grad, query_heads, preferred_element_...  3.11 us
  transfers between devices with their start and end apart: 3, of which 2 were waited for; matrix products, arithmetic and copies ran while one was open for 27% of the time, Pallas kernels for 0%

commit v1 on v0

--- a/solution.py
+++ b/solution.py
@@ -20,15 +20,30 @@
     return (new_global, new_momentum)
 
 
-def outer_update(local_params, global_params, momentum, frag_index):
+def outer_update(local_params, global_params, momentum, frag_index, after):
     chosen = frag_index[0]
     local_sel = lax.dynamic_index_in_dim(local_params[0], chosen, 0, keepdims=False).astype(
         jnp.float32
     )
     outer_old = lax.dynamic_index_in_dim(global_params, chosen, 0, keepdims=False)
     moment_old = lax.dynamic_index_in_dim(momentum, chosen, 0, keepdims=False)
-    summed = lax.psum(local_sel.astype(jnp.bfloat16), "rep").astype(jnp.float32)
+    summed = lax.psum(local_sel.astype(jnp.bfloat16), "rep")
+    summed, after = lax.optimization_barrier((summed, after))
+    summed = summed.astype(jnp.float32)
     return nesterov(outer_old, moment_old, summed)
+
+
+def sibling_pairs(size):
+    return [(t, t ^ 1) for t in range(size)]
+
+
+def chip_shift(size, step):
+    chips = size // 2
+    return [(t, ((t // 2 + step) % chips) * 2 + t % 2) for t in range(size)]
+
+
+def rows_of(array, owner, count):
+    return lax.dynamic_slice_in_dim(array, owner * count, count, 0)
 
 
 def inner_step(queries, keys, values, out_weight, cotangent):
@@ -37,6 +52,18 @@
     heads_here = head_cols // HD
     tokens = queries.shape[1]
     weight_here = out_weight[0]
+    cot_here = cotangent[0]
+    own_rows = cot_here.shape[0]
+    size = lax.axis_size("tp")
+    chips = size // 2
+    me = lax.axis_index("tp")
+    chip, core = me // 2, me % 2
+    pairs = sibling_pairs(size)
+
+    cot_far = [lax.ppermute(cot_here, "tp", chip_shift(size, k)) for k in range(1, chips)]
+    cot_near = lax.ppermute(cot_here, "tp", pairs)
+    weight_near = lax.ppermute(weight_here, "tp", pairs)
+
     query_heads = queries[0].reshape(SEQS, LEN, heads_here, HD)
     key_heads = keys[0].reshape(SEQS, LEN, heads_here, HD)
     value_heads = values[0].reshape(SEQS, LEN, heads_here, HD)
@@ -54,25 +81,50 @@
         "shlm,smhd->slhd", probs_half, value_heads, preferred_element_type=jnp.float32
     )
     context = context.astype(jnp.bfloat16).reshape(tokens, head_cols)
-    context_rows = context
-    branch_out = lax.psum_scatter(
-        jnp.dot(context_rows, weight_here, preferred_element_type=jnp.float32).astype(jnp.bfloat16),
-        "tp",
-        scatter_dimension=0,
-        tiled=True,
+
+    give = jnp.concatenate(
+        [rows_of(context, ((chip + k) % chips) * 2 + 1 - core, own_rows) for k in range(chips)]
     )
-    block_rows = lax.all_gather(cotangent[0], "tp", axis=0, tiled=True)
+    taken = lax.ppermute(give, "tp", pairs)
+    mine = jnp.concatenate(
+        [rows_of(context, ((chip + k) % chips) * 2 + core, own_rows) for k in range(chips)]
+    )
+    both = jnp.concatenate([mine, taken], axis=1)
+    weight_both = jnp.concatenate([weight_here, weight_near], axis=0)
+    far = [
+        jnp.dot(
+            both[k * own_rows : (k + 1) * own_rows], weight_both, preferred_element_type=jnp.float32
+        ).astype(jnp.bfloat16)
+        for k in range(1, chips)
+    ]
+    own = jnp.dot(both[:own_rows], weight_both, preferred_element_type=jnp.float32)
+    far, cot_far, own = lax.optimization_barrier((far, cot_far, own))
+    got = [lax.ppermute(p, "tp", chip_shift(size, k)) for k, p in enumerate(far, 1)]
+    for part in got:
+        own = own + part.astype(jnp.float32)
+    branch_out = own.astype(jnp.bfloat16)
+
+    cot_far_near = [lax.ppermute(c, "tp", pairs) for c in cot_far]
+    blocks = [cot_here, cot_near]
+    owners = [me, chip * 2 + 1 - core]
+    for k in range(1, chips):
+        from_chip = (chip - k + chips) % chips
+        blocks += [cot_far[k - 1], cot_far_near[k - 1]]
+        owners += [from_chip * 2 + core, from_chip * 2 + 1 - core]
+    block_rows = jnp.concatenate(blocks)
+    context_rows = jnp.concatenate([rows_of(context, o, own_rows) for o in owners])
+    weight_grad = lax.dot_general(
+        context_rows, block_rows, (((0,), (0,)), ((), ())), preferred_element_type=jnp.float32
+    ).astype(jnp.bfloat16)
     part_grad = lax.dot_general(
         block_rows, weight_here, (((1,), (1,)), ((), ())), preferred_element_type=jnp.float32
-    )
-    context_acc = part_grad
-    context_rows = context
-    weight_acc = lax.dot_general(
-        context_rows, block_rows, (((0,), (0,)), ((), ())), preferred_element_type=jnp.float32
-    )
-    context_acc, weight_acc = (context_acc, weight_acc)
-    weight_grad = weight_acc.astype(jnp.bfloat16)
-    context_grad = context_acc.astype(jnp.bfloat16).reshape(SEQS, LEN, heads_here, HD)
+    ).astype(jnp.bfloat16)
+    context_grad = jnp.zeros((tokens, head_cols), jnp.bfloat16)
+    for i, o in enumerate(owners):
+        context_grad = lax.dynamic_update_slice_in_dim(
+            context_grad, part_grad[i * own_rows : (i + 1) * own_rows], o * own_rows, 0
+        )
+    context_grad = context_grad.reshape(SEQS, LEN, heads_here, HD)
     probs_grad = jnp.einsum(
         "slhd,smhd->shlm", context_grad, value_heads, preferred_element_type=jnp.float32
     )
@@ -98,7 +150,9 @@
     queries, keys, values, out_weight, cotangent, local_params, global_params, momentum, frag_index
 ):
     results = inner_step(queries, keys, values, out_weight, cotangent)
-    new_global, new_momentum = outer_update(local_params, global_params, momentum, frag_index)
+    new_global, new_momentum = outer_update(
+        local_params, global_params, momentum, frag_index, results[2]
+    )
     return (results[0], results[1], results[2], results[3], results[4], new_global, new_momentum)
 
 

time: 143 us -> 142 us (level)
  waiting for transfers between devices: 86.8 us -> 71.2 us
  starting transfers between devices: 0.12 us -> 5.55 us
  other arithmetic: 1.81 us -> 6.39 us
  local copies, waits for them, and re-layouts: 3.69 us -> 7.3 us
  matrix products: 33.5 us -> 36.7 us
  between operations: 16.4 us -> 14.9 us
    reduce_scatter x1 -> x0, waiting for transfers between devices: 23 us -> none  [inner_step(): lax.psum_scatter(jnp.dot(context_rows, weight_here, preferred_element_typ...]
    ppermute x0 -> x6, waiting for transfers between devices: none -> 22.7 us  [the longest x1 20.9 us: inner_step(): lax.ppermute(cot_here, 'tp', chip_shift(size, k))]
    psum x1, waiting for transfers between devices: 63.3 us -> 48.4 us  [outer_update(): summed = lax.psum(local_sel.astype(jnp.bfloat16), 'rep')]
    ppermute x0 -> x6, starting transfers between devices: none -> 5.51 us  [the longest x1 2.6 us: inner_step(): lax.ppermute(cot_here, 'tp', chip_shift(size, k))]
    broadcast_in_dim x0 -> x1, other arithmetic: none -> 4.33 us  [inner_step(): branch_out[None]]
    dot_general x1 -> x2, matrix products: 7.37 us -> 10.7 us  [the longest x1 6.31 us: inner_step(): jnp.dot(both[:own_rows], weight_both, preferred_element_type=jnp.float32)]
    another operation x3, local copies, waits for them, and re-layouts: 0.35 us -> 3.2 us
    dot_general x1, matrix products: 7.12 us -> 5.27 us  [inner_step(): lax.dot_general(context_rows, block_rows, (((0,), (0,)), ((), ())), prefe...]
  transfers between devices with their start and end apart: 3 -> 7, of which waited for: 2 -> 4; matrix products, arithmetic and copies ran while one was open for 27% -> 29% of each run, Pallas kernels for 0% -> 0%
where the time goes in v1:
time: 142 us
  waiting for transfers between devices  71.2 us (50%)
  matrix products  36.7 us (26%)
  between operations  14.9 us (10%)
  local copies, waits for them, and re-layouts  7.3 us (5%)
  other arithmetic  6.39 us (4%)
  starting transfers between devices  5.55 us (4%)
    psum x1, waiting for transfers between devices, outer_update(): summed = lax.psum(local_sel.astype(jnp.bfloat16), 'rep')  48.4 us
    ppermute x1, waiting for transfers between devices, inner_step(): lax.ppermute(cot_here, 'tp', chip_shift(size, k))  20.9 us
    dot_general x1, matrix products, inner_step(): lax.dot_general(block_rows, weight_here, (((1,), (1,)), ((), ())), prefer...  7.95 us
    dot_general x1, matrix products, inner_step(): jnp.dot(both[:own_rows], weight_both, preferred_element_type=jnp.float32)  6.31 us
    dot_general x1, matrix products, inner_step(): lax.dot_general(context_rows, block_rows, (((0,), (0,)), ((), ())), prefe...  5.27 us
    dot_general x1, matrix products, inner_step(): jnp.dot(both[k * own_rows:(k + 1) * own_rows], weight_both, preferred_ele...  4.43 us
    broadcast_in_dim x1, other arithmetic, inner_step(): branch_out[None]  4.33 us
    dot_general x1, matrix products, inner_step(): jnp.einsum('shlm,smhd->slhd', score_grad, key_heads, preferred_element_ty...  3.24 us
  transfers between devices with their start and end apart: 7, of which 4 were waited for; matrix products, arithmetic and copies ran while one was open for 29% of the time, Pallas kernels for 0%

profile of v1, /device:TPU:0, one launch (start us, length us, event | category | flops | bytes accessed | tf_op | source)
XLA Modules:
  0.0 141.9 jit_solution(3274658239823380483)
XLA Ops:
  7.2 0.0 copy-start
  7.2 0.0 all-reduce.2.cloned.1.call-start
  7.2 0.5 collective-permute-start.1
  7.7 2.6 %collective-permute-start.2 = (bf16[128,7168]{1,0:T(8,128)(2,1)}, bf16[128,7168]{1,0:T(8,128)(2,1)}, u32[]{:S(2)}, u32[]{:S(2)}) collective-permute-start(bf16[128,7168]{1,0:T(8,128)(2,1)} %bitcast.81), channel_id=1, source_target_pairs={{0,2},{1,3},{2,0},{3,1},{4,6},{5,7},{6,4},{7,5},{8,10},{9,11},{10,... | collective-permute-start | bytes 5505032 | tf_op jit(solution)/shard_map/ppermute | solution.py:63
  10.3 1.0 reshape.115
  11.4 1.1 copy.35
  12.5 1.1 copy.36
  13.6 0.1 iota_compare_fusion
  13.7 0.0 copy-start.1
  13.7 2.3 %fusion.55 = (f32[2,512]{1,0:T(2,128)S(1)}, f32[2,512,512]{1,2,0:T(8,128)}) fusion(pred[512,512]{0,1:T(8,128)(4,1)S(1)} %iota_compare_fusion, bf16[512,2,128]{0,2,1:T(8,128)(2,1)S(1)} %bitcast.67, bf16[512,2,128]{0,2,1:T(8,128)(2,1)S(1)} %bitcast.71), kind=kOutput, calls=%fused_computation.73 | convolution fusion | flops 136315392 | bytes 2887680 | tf_op jit(solution)/shard_map/sub | solution.py:77
  16.0 0.0 copy-done.1
  16.0 0.0 copy-start.5
  16.0 1.3 convolution_convert_fusion.2
  17.3 0.7 constant_dynamic-slice_fusion.1
  18.1 0.2 collective-permute-start
  18.3 0.0 copy-done.5
  18.3 0.4 collective-permute-start.4
  18.7 0.8 collective-permute-done
  19.6 0.0 copy-start.4
  19.6 0.0 collective-permute-done.1
  19.6 6.3 %fusion.3 = f32[128,7168]{1,0:T(8,128)} fusion(bf16[256,7168]{1,0:T(8,128)(2,1)} %collective-permute-done.1, bf16[256,7168]{1,0:T(8,128)(2,1)} %bitcast.79, bf16[256,512]{0,1:T(8,128)(2,1)S(1)} %pad_maximum_fusion.8), kind=kOutput, calls=%fused_computation.7 | convolution fusion | flops 954204160 | bytes 11141120 | tf_op jit(solution)/shard_map/dot_general | solution.py:100
  25.9 0.0 copy-done.4
  25.9 4.4 %convolution_convert_fusion.1 = bf16[128,7168]{1,0:T(8,128)(2,1)} fusion(bf16[256,7168]{1,0:T(8,128)(2,1)} %collective-permute-done.1, bf16[256,7168]{1,0:T(8,128)(2,1)S(1)} %bitcast.80, bf16[256,512]{0,1:T(8,128)(2,1)S(1)} %pad_maximum_fusion.8), kind=kOutput, calls=%fused_computation.4 | convolution fusion | flops 955121664 | bytes 9306112 | tf_op jit(solution)/shard_map/dot_general | solution.py:95
  30.3 20.9 %collective-permute-done.2 = bf16[128,7168]{1,0:T(8,128)(2,1)} collective-permute-done((bf16[128,7168]{1,0:T(8,128)(2,1)}, bf16[128,7168]{1,0:T(8,128)(2,1)}, u32[]{:S(2)}, u32[]{:S(2)}) %collective-permute-start.2) | collective-permute-done | bytes 1835040 | tf_op jit(solution)/shard_map/ppermute | solution.py:63
  51.3 0.0 collective-permute-start.5
  51.9 0.0 copy-done
  51.9 0.7 dynamic-slice_bitcast_fusion
  52.6 0.0 all-reduce.2.cloned.1.call-update
  52.6 1.8 %collective-permute-start.3 = (bf16[128,7168]{1,0:T(8,128)(2,1)}, bf16[128,7168]{1,0:T(8,128)(2,1)}, u32[]{:S(2)}, u32[]{:S(2)}) collective-permute-start(bf16[128,7168]{1,0:T(8,128)(2,1)} %convolution_convert_fusion.1), channel_id=1, source_target_pairs={{0,2},{1,3},{2,0},{3,1},{4,6},{5,7},{6,4},{7,5},{8,10},{9,11},{10,... | collective-permute-start | bytes 5505032 | tf_op jit(solution)/shard_map/ppermute | solution.py:102
  54.4 0.0 collective-permute-done.4
  54.4 0.9 collective-permute-done.5
  55.4 7.9 %fusion.22 = bf16[512,256]{0,1:T(8,128)(2,1)S(1)} fusion(bf16[128,7168]{1,0:T(8,128)(2,1)} %collective-permute-done.5, bf16[128,7168]{1,0:T(8,128)(2,1)} %collective-permute-done.2, bf16[128,7168]{1,0:T(8,128)(2,1)} %collective-permute-done.4, bf16[128,7168]{1,0:T(8,128)(2,1)S(1)} %bitcast.83, bf16[1,256,7168]{2,1,0:T(8,128)(2,1)} %param.12), kind=kOutput, calls=%fused_computation.23 | convolution fusion | flops 1908539392 | bytes 11272192 | tf_op jit(solution)/shard_map/dot_general | solution.py:119
  63.5 0.4 fusion.38
  63.9 2.3 %convolution_convert_fusion.3 = bf16[2,128,512]{2,1,0:T(8,128)(2,1)S(1)} fusion(bf16[512,2,128]{0,2,1:T(8,128)(2,1)S(1)} %bitcast.65, f32[2,512]{1,0:T(2,128)S(1)} %get-tuple-element.30, pred[512,512]{0,1:T(8,128)(4,1)} %copy-done.1, bf16[512,2,128]{0,2,1:T(8,128)(2,1)S(1)} %bitcast.69, bf16[512,2,128]{0,2,1:T(8,128)(2,1)S(1)} %bitcast.73), kind=kOutput, calls=%fused_computation.22 | convolution fusion | flops 271189504 | bytes 1314816 | tf_op jit(solution)/shard_map/shlm,slhd->smhd/dot_general | solution.py:139
  66.2 3.2 %fusion.16 = bf16[2,512,128]{1,2,0:T(8,128)(2,1)S(1)} fusion(bf16[512,2,128]{0,2,1:T(8,128)(2,1)S(1)} %bitcast.74, f32[2,512,512]{1,2,0:T(8,128)S(1)} %fusion.38, f32[2,512,512]{1,2,0:T(8,128)} %get-tuple-element.31, f32[2,512]{1,0:T(2,128)S(1)} %get-tuple-element.30), kind=kOutput, calls=%fused_computation.19 | convolution fusion | flops 138020352 | bytes 4722688 | tf_op jit(solution)/shard_map/shlm,smhd->slhd/dot_general | solution.py:133
  69.5 3.1 %fusion.19 = bf16[2,512,128]{1,2,0:T(8,128)(2,1)S(1)} fusion(bf16[512,2,128]{0,2,1:T(8,128)(2,1)S(1)} %bitcast.70, f32[2,512,512]{1,2,0:T(8,128)S(1)} %fusion.38, f32[2,512,512]{1,2,0:T(8,128)} %get-tuple-element.31, f32[2,512]{1,0:T(2,128)S(1)} %get-tuple-element.30), kind=kOutput, calls=%fused_computation.20 | convolution fusion | flops 138020352 | bytes 4722688 | tf_op jit(solution)/shard_map/shlm,slhd->smhd/dot_general | solution.py:136
  72.6 0.8 copy.27
  73.4 0.8 copy.28
  74.3 0.8 copy.29
  75.1 48.4 %all-reduce.2.cloned.1.call-done = bf16[8,7168]{1,0:T(8,128)(2,1)} async-done(((bf16[8,7168]{1,0:T(8,128)(2,1)}), bf16[8,7168]{1,0:T(8,128)(2,1)}) %all-reduce.2.cloned.1.call-update) | async-done | bytes 114704 | tf_op jit(solution)/shard_map/psum | solution.py:30
  123.5 1.9 %bitcast_subtract_fusion = (f32[8,7168]{1,0:T(8,128)}, f32[8,7168]{1,0:T(8,128)}) fusion(bf16[8,7168]{1,0:T(8,128)(2,1)} %all-reduce.2.cloned.1.call-done, f32[2,8,7168]{2,1,0:T(8,128)} %param.15, s32[]{:T(128)S(6)} %select_n.72, f32[2,8,7168]{2,1,0:T(8,128)} %param.16), kind=kLoop, calls=%fused_computation.45 | loop fusion | flops 516096 | bytes 1032196 | tf_op jit(solution)/shard_map/sub | solution.py:19
  125.5 0.0 copy-start.2
  125.5 0.0 copy-start.3
  125.5 0.0 copy-start.6
  125.5 0.0 collective-permute-done.3
  125.5 4.3 %fusion.8 = bf16[1,128,7168]{2,1,0:T(8,128)(2,1)} fusion(f32[128,7168]{1,0:T(8,128)} %fusion.3, bf16[128,7168]{1,0:T(8,128)(2,1)} %collective-permute-done.3), kind=kLoop, calls=%fused_computation.15 | loop fusion | flops 2752512 | bytes 7340032 | tf_op jit(solution)/shard_map/broadcast_in_dim | solution.py:146
  129.8 0.0 copy-done.2
  129.8 0.0 copy-done.3
  129.8 0.0 copy-done.6
  129.8 5.3 %fusion.2 = bf16[1,256,7168]{2,1,0:T(8,128)(2,1)} fusion(bf16[128,7168]{1,0:T(8,128)(2,1)} %collective-permute-done.5, bf16[128,7168]{1,0:T(8,128)(2,1)} %collective-permute-done.2, bf16[128,7168]{1,0:T(8,128)(2,1)} %collective-permute-done.4, bf16[128,7168]{1,0:T(8,128)(2,1)S(1)} %bitcast.84, bf16[128,256]{0,1:T(8,128)(2,1)S(1)} %get-tuple-element.26, ...), kind=kOutput, calls=%fused_computation.3 | convolution fusion | flops 1911291904 | bytes 11272192 | tf_op jit(solution)/shard_map/dot_general | solution.py:116
  (7 shorter events, 0.2 us)
Async XLA Ops:
  7.2 44.8 %copy-start = (bf16[1,2,8,7168]{3,2,1,0:T(8,128)(2,1)S(1)}, bf16[1,2,8,7168]{3,2,1,0:T(8,128)(2,1)}, u32[]{:S(2)}) copy-start(bf16[1,2,8,7168]{3,2,1,0:T(8,128)(2,1)} %param.14) | copy-start | bytes 688132
  7.2 116.4 %all-reduce.2.cloned.1.call-start = ((), (), s32[]{:S(2)}) async-start(), calls=%async_computation | async-start | bytes 229376 | tf_op jit(solution)/shard_map/psum | solution.py:30
  7.2 12.3 %collective-permute-start.1 = (bf16[256,7168]{1,0:T(8,128)(2,1)}, bf16[256,7168]{1,0:T(8,128)(2,1)}, u32[]{:S(2)}, u32[]{:S(2)}) collective-permute-start(bf16[256,7168]{1,0:T(8,128)(2,1)} %bitcast.78), channel_id=1, source_target_pairs={{0,1},{1,0},{2,3},{3,2},{4,5},{5,4},{6,7},{7,6},{8,9},{9,8},{10,11... | collective-permute-start | bytes 11010056 | tf_op jit(solution)/shard_map/ppermute | solution.py:65
  7.7 43.5 %collective-permute-start.2 = (bf16[128,7168]{1,0:T(8,128)(2,1)}, bf16[128,7168]{1,0:T(8,128)(2,1)}, u32[]{:S(2)}, u32[]{:S(2)}) collective-permute-start(bf16[128,7168]{1,0:T(8,128)(2,1)} %bitcast.81), channel_id=1, source_target_pairs={{0,2},{1,3},{2,0},{3,1},{4,6},{5,7},{6,4},{7,5},{8,10},{9,11},{10,... | collective-permute-start | bytes 5505032 | tf_op jit(solution)/shard_map/ppermute | solution.py:63
  13.7 2.4 %copy-start.1 = (pred[512,512]{0,1:T(8,128)(4,1)}, pred[512,512]{0,1:T(8,128)(4,1)S(1)}, u32[]{:S(2)}) copy-start(pred[512,512]{0,1:T(8,128)(4,1)S(1)} %iota_compare_fusion) | copy-start | bytes 786436
  16.0 2.3 %copy-start.5 = (bf16[1,128,7168]{2,1,0:T(8,128)(2,1)S(1)}, bf16[1,128,7168]{2,1,0:T(8,128)(2,1)}, u32[]{:S(2)}) copy-start(bf16[1,128,7168]{2,1,0:T(8,128)(2,1)} %param.13) | copy-start | bytes 5505028
  18.1 1.4 collective-permute-start
  18.3 36.1 %collective-permute-start.4 = (bf16[128,7168]{1,0:T(8,128)(2,1)S(1)}, bf16[128,7168]{1,0:T(8,128)(2,1)}, u32[]{:S(2)}, u32[]{:S(2)}) collective-permute-start(bf16[128,7168]{1,0:T(8,128)(2,1)S(1)} %bitcast.82), channel_id=1, source_target_pairs={{0,1},{1,0},{2,3},{3,2},{4,5},{5,4},{6,7},{7,6},{8,9},{9,8},{10,11... | collective-permute-start | bytes 5505032 | tf_op jit(solution)/shard_map/ppermute | solution.py:64
  19.6 6.3 %copy-start.4 = (bf16[1,256,7168]{2,1,0:T(8,128)(2,1)S(1)}, bf16[1,256,7168]{2,1,0:T(8,128)(2,1)}, u32[]{:S(2)}) copy-start(bf16[1,256,7168]{2,1,0:T(8,128)(2,1)} %param.12) | copy-start | bytes 11010052
  51.3 4.1 %collective-permute-start.5 = (bf16[128,7168]{1,0:T(8,128)(2,1)}, bf16[128,7168]{1,0:T(8,128)(2,1)}, u32[]{:S(2)}, u32[]{:S(2)}) collective-permute-start(bf16[128,7168]{1,0:T(8,128)(2,1)} %collective-permute-done.2), channel_id=1, source_target_pairs={{0,1},{1,0},{2,3},{3,2},{4,5},{5,4},{6,7},{7,6},{8,9},{9,8},{10,11... | collective-permute-start | bytes 5505032 | tf_op jit(solution)/shard_map/ppermute | solution.py:107
  52.6 72.9 %collective-permute-start.3 = (bf16[128,7168]{1,0:T(8,128)(2,1)}, bf16[128,7168]{1,0:T(8,128)(2,1)}, u32[]{:S(2)}, u32[]{:S(2)}) collective-permute-start(bf16[128,7168]{1,0:T(8,128)(2,1)} %convolution_convert_fusion.1), channel_id=1, source_target_pairs={{0,2},{1,3},{2,0},{3,1},{4,6},{5,7},{6,4},{7,5},{8,10},{9,11},{10,... | collective-permute-start | bytes 5505032 | tf_op jit(solution)/shard_map/ppermute | solution.py:102
  125.5 4.3 %copy-start.2 = (bf16[128,256]{0,1:T(8,128)(2,1)S(1)}, bf16[128,256]{0,1:T(8,128)(2,1)}, u32[]{:S(2)}) copy-start(bf16[128,256]{0,1:T(8,128)(2,1)} %get-tuple-element.24) | copy-start | bytes 196612
  125.5 4.3 %copy-start.3 = (bf16[128,256]{0,1:T(8,128)(2,1)S(1)}, bf16[128,256]{0,1:T(8,128)(2,1)}, u32[]{:S(2)}) copy-start(bf16[128,256]{0,1:T(8,128)(2,1)} %get-tuple-element.25) | copy-start | bytes 196612
  125.5 4.3 %copy-start.6 = (bf16[1,128,7168]{2,1,0:T(8,128)(2,1)S(1)}, bf16[1,128,7168]{2,1,0:T(8,128)(2,1)}, u32[]{:S(2)}) copy-start(bf16[1,128,7168]{2,1,0:T(8,128)(2,1)} %param.13) | copy-start | bytes 5505028
Sparse Core Ops, SparseCore 0:
  52.7 70.7 all-reduce.1

commit v2 on v1

v2 whole, which is shorter than its diff:
```python
import jax
import jax.numpy as jnp
from jax import lax
from jax.experimental import pallas as pl
from jax.experimental.pallas import tpu as pltpu
from jax.sharding import PartitionSpec as P

HD = 128
LEN = 512
SEQS = 1


outer_momentum = 0.9
outer_rate = 0.7


def nesterov(outer_old, moment_old, summed):
    average = summed / lax.axis_size("rep")
    pseudo_grad = outer_old - average
    new_momentum = outer_momentum * moment_old + pseudo_grad
    new_global = outer_old - outer_rate * (outer_momentum * new_momentum + pseudo_grad)
    return (new_global, new_momentum)


def sum_replicas(local_sel):
    size = lax.axis_size("rep")
    others = [
        lax.ppermute(local_sel, "rep", [(r, (r + k) % size) for r in range(size)])
        for k in range(1, size)
    ]
    total = local_sel.astype(jnp.float32)
    for other in others:
        total = total + other.astype(jnp.float32)
    return total


def outer_update(summed, global_params, momentum, frag_index):
    chosen = frag_index[0]
    outer_old = lax.dynamic_index_in_dim(global_params, chosen, 0, keepdims=False)
    moment_old = lax.dynamic_index_in_dim(momentum, chosen, 0, keepdims=False)
    return nesterov(outer_old, moment_old, summed)


def sibling_pairs(size):
    return [(t, t ^ 1) for t in range(size)]


def chip_shift(size, step):
    chips = size // 2
    return [(t, ((t // 2 + step) % chips) * 2 + t % 2) for t in range(size)]


def rows_of(array, owner, count):
    return lax.dynamic_slice_in_dim(array, owner * count, count, 0)


def dot(a, b, over):
    return lax.dot_general(a, b, ((over[:1], over[1:]), ((), ())), preferred_element_type=jnp.float32)


def vmem(mib):
    return pltpu.CompilerParams(vmem_limit_bytes=mib * 2**20)


def cost(flops, *arrays):
    moved = sum(a.size * a.dtype.itemsize for a in arrays)
    return pl.CostEstimate(flops=flops, bytes_accessed=moved, transcendentals=0)


def column_block(cols):
    return 1024 if cols % 1024 == 0 else cols


def softmax_rows(query, key, first):
    scores = dot(query, key, (1, 1)) * HD ** (-0.5)
    row = lax.broadcasted_iota(jnp.int32, scores.shape, 0) + first
    col = lax.broadcasted_iota(jnp.int32, scores.shape, 1)
    scores = jnp.where(row >= col, scores, -1e30)
    weights = jnp.exp(scores - jnp.max(scores, axis=-1, keepdims=True))
    return weights / jnp.sum(weights, axis=-1, keepdims=True)


ROWS = 256


def forward_kernel(q_ref, k_ref, v_ref, out_ref):
    for first in range(0, LEN, ROWS):
        end = first + ROWS
        probs = softmax_rows(q_ref[first:end, :], k_ref[:end, :], first)
        out_ref[first:end, :] = dot(probs.astype(jnp.bfloat16), v_ref[:end, :], (1, 0)).astype(
            jnp.bfloat16
        )


def backward_kernel(q_ref, k_ref, v_ref, g_ref, dq_ref, dk_ref, dv_ref, dk_acc, dv_acc):
    dk_acc[...] = jnp.zeros_like(dk_acc)
    dv_acc[...] = jnp.zeros_like(dv_acc)
    for first in range(0, LEN, ROWS):
        end = first + ROWS
        query, grad = q_ref[first:end, :], g_ref[first:end, :]
        probs = softmax_rows(query, k_ref[:end, :], first)
        probs_grad = dot(grad, v_ref[:end, :], (1, 1))
        inner = jnp.sum(probs * probs_grad, axis=-1, keepdims=True)
        score_grad = (probs * (probs_grad - inner) * HD ** (-0.5)).astype(jnp.bfloat16)
        dq_ref[first:end, :] = dot(score_grad, k_ref[:end, :], (1, 0)).astype(jnp.bfloat16)
        dk_acc[:end, :] += dot(score_grad, query, (0, 0))
        dv_acc[:end, :] += dot(probs.astype(jnp.bfloat16), grad, (0, 0))
    dk_ref[...] = dk_acc[...].astype(jnp.bfloat16)
    dv_ref[...] = dv_acc[...].astype(jnp.bfloat16)


def attention_forward(query, key, value):
    spec = pl.BlockSpec((LEN, HD), lambda h: (0, h))
    return pl.pallas_call(
        forward_kernel,
        grid=(query.shape[1] // HD,),
        in_specs=[spec] * 3,
        out_specs=spec,
        out_shape=jax.ShapeDtypeStruct(query.shape, jnp.bfloat16),
        compiler_params=vmem(32),
    )(query, key, value)


def attention_backward(query, key, value, grad):
    spec = pl.BlockSpec((LEN, HD), lambda h: (0, h))
    return pl.pallas_call(
        backward_kernel,
        grid=(query.shape[1] // HD,),
        in_specs=[spec] * 4,
        out_specs=[spec] * 3,
        out_shape=[jax.ShapeDtypeStruct(query.shape, jnp.bfloat16)] * 3,
        scratch_shapes=[pltpu.VMEM((LEN, HD), jnp.float32)] * 2,
        compiler_params=vmem(32),
        cost_estimate=cost(10 * LEN * query.size, query, key, value, grad, query, key, value),
    )(query, key, value, grad)


def branch_kernel(mine_ref, taken_ref, here_ref, near_ref, *out_refs):
    total = dot(mine_ref[...], here_ref[...], (1, 0)) + dot(taken_ref[...], near_ref[...], (1, 0))
    rows = out_refs[0].shape[0]
    for k, out in enumerate(out_refs):
        out[...] = total[k * rows : (k + 1) * rows].astype(out.dtype)


def branch_parts(mine, taken, here, near, chips):
    rows, cols = mine.shape[0] // chips, here.shape[1]
    block = column_block(cols)
    whole = pl.BlockSpec(mine.shape, lambda i: (0, 0))
    weight = pl.BlockSpec((here.shape[0], block), lambda i: (0, i))
    out = jax.ShapeDtypeStruct((rows, cols), jnp.bfloat16)
    return pl.pallas_call(
        branch_kernel,
        grid=(cols // block,),
        in_specs=[whole, whole, weight, weight],
        out_specs=[pl.BlockSpec((rows, block), lambda i: (0, i))] * chips,
        out_shape=[out] * chips,
        compiler_params=vmem(32),
    )(mine, taken, here, near)


def grads_kernel(*refs):
    context_ref, weight_ref, *cot_refs = refs[:-3]
    wgrad_ref, cgrad_ref, total = refs[-3:]
    step = pl.program_id(0)

    @pl.when(step == 0)
    def _():
        total[...] = jnp.zeros_like(total)

    cot = jnp.concatenate([c[...] for c in cot_refs], axis=0)
    wgrad_ref[...] = dot(context_ref[...], cot, (1, 0)).astype(wgrad_ref.dtype)
    total[...] += dot(cot, weight_ref[...], (1, 1))

    @pl.when(step == pl.num_programs(0) - 1)
    def _():
        cgrad_ref[...] = total[...].astype(cgrad_ref.dtype)


def projection_grads(context_t, weight, cots):
    features, tokens = context_t.shape
    rows, cols = cots[0].shape
    block = column_block(cols)
    column = pl.BlockSpec((features, block), lambda i: (0, i))
    out = [
        jax.ShapeDtypeStruct((features, cols), jnp.bfloat16),
        jax.ShapeDtypeStruct((tokens, features), jnp.bfloat16),
    ]
    return pl.pallas_call(
        grads_kernel,
        grid=(cols // block,),
        in_specs=[pl.BlockSpec((features, tokens), lambda i: (0, 0)), column]
        + [pl.BlockSpec((rows, block), lambda i: (0, i))] * len(cots),
        out_specs=[column, pl.BlockSpec((tokens, features), lambda i: (0, 0))],
        out_shape=out,
        scratch_shapes=[pltpu.VMEM((tokens, features), jnp.float32)],
        compiler_params=vmem(32),
        cost_estimate=cost(4 * tokens * features * cols, context_t, weight, *cots, *out),
    )(context_t, weight, *cots)


def add_kernel(*refs):
    total = refs[0][...].astype(jnp.float32)
    for part in refs[1:-1]:
        total = total + part[...].astype(jnp.float32)
    refs[-1][...] = total.astype(refs[-1].dtype)


def add_parts(parts):
    rows, cols = parts[0].shape
    block = column_block(cols)
    spec = pl.BlockSpec((rows, block), lambda i: (0, i))
    return pl.pallas_call(
        add_kernel,
        grid=(cols // block,),
        in_specs=[spec] * len(parts),
        out_specs=spec,
        out_shape=jax.ShapeDtypeStruct((rows, cols), jnp.bfloat16),
    )(*parts)


def inner_step(queries, keys, values, out_weight, cotangent, local_sel):
    weight_here = out_weight[0]
    cot_here = cotangent[0]
    own_rows = cot_here.shape[0]
    size = lax.axis_size("tp")
    chips = size // 2
    me = lax.axis_index("tp")
    chip, core = me // 2, me % 2
    pairs = sibling_pairs(size)

    cot_far = [lax.ppermute(cot_here, "tp", chip_shift(size, k)) for k in range(1, chips)]
    cot_near = lax.ppermute(cot_here, "tp", pairs)
    weight_near = lax.ppermute(weight_here, "tp", pairs)

    context = attention_forward(queries[0], keys[0], values[0])
    summed = sum_replicas(local_sel)

    give = jnp.concatenate(
        [rows_of(context, ((chip + k) % chips) * 2 + 1 - core, own_rows) for k in range(chips)]
    )
    taken = lax.ppermute(give, "tp", pairs)
    mine = jnp.concatenate(
        [rows_of(context, ((chip + k) % chips) * 2 + core, own_rows) for k in range(chips)]
    )
    own, *far = branch_parts(mine, taken, weight_here, weight_near, chips)
    far, cot_far, own, summed = lax.optimization_barrier((far, cot_far, own, summed))
    got = [lax.ppermute(p, "tp", chip_shift(size, k)) for k, p in enumerate(far, 1)]

    cot_far_near = [lax.ppermute(c, "tp", pairs) for c in cot_far]
    blocks = [cot_here, cot_near]
    owners = [me, chip * 2 + 1 - core]
    for k in range(1, chips):
        from_chip = (chip - k + chips) % chips
        blocks += [cot_far[k - 1], cot_far_near[k - 1]]
        owners += [from_chip * 2 + core, from_chip * 2 + 1 - core]
    context_rows = jnp.concatenate([rows_of(context, o, own_rows) for o in owners])
    weight_grad, part_grad = projection_grads(context_rows.T, weight_here, blocks)
    context_grad = jnp.zeros_like(context)
    for i, o in enumerate(owners):
        context_grad = lax.dynamic_update_slice_in_dim(
            context_grad, part_grad[i * own_rows : (i + 1) * own_rows], o * own_rows, 0
        )
    shaped = attention_backward(queries[0], keys[0], values[0], context_grad)
    got, weight_grad, shaped = lax.optimization_barrier((got, weight_grad, shaped))
    branch_out = add_parts([own] + got)
    return (branch_out[None], weight_grad[None], *[g[None] for g in shaped], summed)


def shards(
    queries, keys, values, out_weight, cotangent, local_params, global_params, momentum, frag_index
):
    local_sel = lax.dynamic_index_in_dim(local_params[0], frag_index[0], 0, keepdims=False)
    *results, summed = inner_step(queries, keys, values, out_weight, cotangent, local_sel)
    new_global, new_momentum = outer_update(summed, global_params, momentum, frag_index)
    return (results[0], results[1], results[2], results[3], results[4], new_global, new_momentum)


def solution(mesh):
    placed = (
        P("rep", None, "tp"),
        P("rep", None, "tp"),
        P("rep", None, "tp"),
        P("rep", "tp", None),
        P("rep", "tp", None),
        P("rep", None, "tp", None),
        P(None, "tp", None),
        P(None, "tp", None),
        P(),
    )
    return jax.shard_map(
        shards,
        mesh=mesh,
        in_specs=placed,
        out_specs=(
            P("rep", "tp", None),
            P("rep", "tp", None),
            P("rep", None, "tp"),
            P("rep", None, "tp"),
            P("rep", None, "tp"),
            P("tp", None),
            P("tp", None),
        ),
        check_vma=False,
    )
```

time: 142 us -> 101 us (0.71)
  matrix products: 36.7 us -> 0 us
  waiting for transfers between devices: 71.2 us -> 38.7 us
  Pallas kernels: 0 us -> 26.7 us
  starting transfers between devices: 5.55 us -> 20.7 us
  between operations: 14.9 us -> 1.56 us
  other arithmetic: 6.39 us -> 1.03 us
  local copies, waits for them, and re-layouts: 7.3 us -> 11.3 us
    psum x1 -> x0, waiting for transfers between devices: 48.4 us -> none  [outer_update(): summed = lax.psum(local_sel.astype(jnp.bfloat16), 'rep')]
    dot_general x9 -> x0, matrix products: 34.3 us -> none  [the longest x1 7.95 us: inner_step(): lax.dot_general(block_rows, weight_here, (((1,), (1,)), ((), ())), prefer...]
    pallas_call x0 -> x5, Pallas kernels: none -> 26.7 us  [the longest x1 8.85 us: projection_grads(): pl.pallas_call(grads_kernel, grid=(cols // block,), in_specs=[pl.BlockSpe...]
    ppermute x1, waiting for transfers between devices: 0.01 us -> 24.1 us  [inner_step(): lax.ppermute(p, 'tp', chip_shift(size, k))]
    ppermute x0 -> x7, starting transfers between devices: none -> 16.5 us  [sum_replicas(): lax.ppermute(local_sel, 'rep', [(r, (r + k) % size) for r in range(size)])]
    ppermute x1, waiting for transfers between devices: 20.9 us -> 5.24 us  [inner_step(): lax.ppermute(cot_here, 'tp', chip_shift(size, k))]
    unnamed x17 -> x34, local copies, waits for them, and re-layouts: 2.56 us -> 10.1 us
    ppermute x0 -> x7, waiting for transfers between devices: none -> 6.69 us  [sum_replicas(): lax.ppermute(local_sel, 'rep', [(r, (r + k) % size) for r in range(size)])]
  transfers between devices with their start and end apart: 7 -> 13, of which waited for: 4 -> 6; matrix products, arithmetic and copies ran while one was open for 29% -> 3% of each run, Pallas kernels for 0% -> 21%
where the time goes in v2:
time: 101 us; the launch traced here: 99.9 us
  waiting for transfers between devices  38.7 us (38%)
  Pallas kernels  26.7 us (26%)
  starting transfers between devices  20.7 us (20%)
  local copies, waits for them, and re-layouts  11.3 us (11%)
  between operations  1.56 us (2%)
  other arithmetic  1.03 us (1%)
    ppermute x1, waiting for transfers between devices, inner_step(): lax.ppermute(p, 'tp', chip_shift(size, k))  24.1 us
    ppermute x7, starting transfers between devices, sum_replicas(): lax.ppermute(local_sel, 'rep', [(r, (r + k) % size) for r in range(size)])  16.5 us
    unnamed x34, local copies, waits for them, and re-layouts  10.1 us
    pallas_call x1, Pallas kernels, projection_grads(): pl.pallas_call(grads_kernel, grid=(cols // block,), in_specs=[pl.BlockSpe...  8.85 us
    ppermute x7, waiting for transfers between devices, sum_replicas(): lax.ppermute(local_sel, 'rep', [(r, (r + k) % size) for r in range(size)])  6.69 us
    pallas_call x1, Pallas kernels, branch_parts(): pl.pallas_call(branch_kernel, grid=(cols // block,), in_specs=[whole, who...  6.29 us
    pallas_call x1, Pallas kernels, add_parts(): pl.pallas_call(add_kernel, grid=(cols // block,), in_specs=[spec] * len(p...  5.57 us
    ppermute x1, waiting for transfers between devices, inner_step(): lax.ppermute(cot_here, 'tp', chip_shift(size, k))  5.24 us
  transfers between devices with their start and end apart: 13, of which 6 were waited for; matrix products, arithmetic and copies ran while one was open for 3% of the time, Pallas kernels for 21%

profile of v2, /device:TPU:0, one launch (start us, length us, event | category | flops | bytes accessed | tf_op | source)
XLA Modules:
  0.0 99.9 jit_solution(7415858293855186373)
XLA Ops:
  0.6 0.0 copy-start.11
  0.6 0.5 collective-permute-start.1
  1.8 0.9 dynamic-slice_bitcast_fusion
  2.7 2.5 %collective-permute-start.3 = (bf16[8,7168]{1,0:T(8,128)(2,1)S(1)}, bf16[8,7168]{1,0:T(8,128)(2,1)S(1)}, u32[]{:S(2)}, u32[]{:S(2)}) collective-permute-start(bf16[8,7168]{1,0:T(8,128)(2,1)S(1)} %dynamic-slice_bitcast_fusion), channel_id=1, source_target_pairs={{0,4},{4,8},{8,12},{12,16},{16,20},{20,24},{24,28},{28,0},{1,5},{5... | collective-permute-start | bytes 344072 | tf_op jit(solution)/shard_map/ppermute | solution.py:28
  5.3 1.6 %collective-permute-start.4 = (bf16[8,7168]{1,0:T(8,128)(2,1)S(1)}, bf16[8,7168]{1,0:T(8,128)(2,1)S(1)}, u32[]{:S(2)}, u32[]{:S(2)}) collective-permute-start(bf16[8,7168]{1,0:T(8,128)(2,1)S(1)} %dynamic-slice_bitcast_fusion), channel_id=1, source_target_pairs={{0,8},{4,12},{8,16},{12,20},{16,24},{20,28},{24,0},{28,4},{1,9},{5... | collective-permute-start | bytes 344072 | tf_op jit(solution)/shard_map/ppermute | solution.py:28
  6.8 2.6 %collective-permute-start.5 = (bf16[8,7168]{1,0:T(8,128)(2,1)S(1)}, bf16[8,7168]{1,0:T(8,128)(2,1)S(1)}, u32[]{:S(2)}, u32[]{:S(2)}) collective-permute-start(bf16[8,7168]{1,0:T(8,128)(2,1)S(1)} %dynamic-slice_bitcast_fusion), channel_id=1, source_target_pairs={{0,12},{4,16},{8,20},{12,24},{16,28},{20,0},{24,4},{28,8},{1,13},{... | collective-permute-start | bytes 344072 | tf_op jit(solution)/shard_map/ppermute | solution.py:28
  9.4 1.5 %collective-permute-start.2 = (bf16[128,7168]{1,0:T(8,128)(2,1)}, bf16[128,7168]{1,0:T(8,128)(2,1)}, u32[]{:S(2)}, u32[]{:S(2)}) collective-permute-start(bf16[128,7168]{1,0:T(8,128)(2,1)} %bitcast.40), channel_id=1, source_target_pairs={{0,2},{1,3},{2,0},{3,1},{4,6},{5,7},{6,4},{7,5},{8,10},{9,11},{10,... | collective-permute-start | bytes 5505032 | tf_op jit(solution)/shard_map/ppermute | solution.py:231
  10.9 0.0 copy-start.3
  10.9 0.9 copy-done.3
  11.9 0.0 copy-start.5
  11.9 0.9 copy-done.5
  12.8 0.0 copy-start.7
  12.8 0.9 copy-done.7
  13.8 0.0 copy-start.9
  13.8 2.1 %shard_map.144 = bf16[512,256]{1,0:T(8,128)(2,1)S(1)} custom-call(bf16[512,256]{1,0:T(8,128)(2,1)S(1)} %bitcast.34, bf16[512,256]{1,0:T(8,128)(2,1)S(1)} %bitcast.36, bf16[512,256]{1,0:T(8,128)(2,1)S(1)} %bitcast.38), custom_call_target="tpu_custom_call" | custom-call | tf_op jit(solution)/shard_map/pallas_call | solution.py:114
  16.0 0.1 copy.26
  16.1 0.1 copy.27
  16.2 0.1 copy.24
  16.3 0.1 copy.25
  16.5 0.0 collective-permute-done.3
  16.5 1.3 %collective-permute-start.6 = (bf16[8,7168]{1,0:T(8,128)(2,1)S(1)}, bf16[8,7168]{1,0:T(8,128)(2,1)S(1)}, u32[]{:S(2)}, u32[]{:S(2)}) collective-permute-start(bf16[8,7168]{1,0:T(8,128)(2,1)S(1)} %dynamic-slice_bitcast_fusion), channel_id=1, source_target_pairs={{0,16},{4,20},{8,24},{12,28},{16,0},{20,4},{24,8},{28,12},{1,17},{... | collective-permute-start | bytes 344072 | tf_op jit(solution)/shard_map/ppermute | solution.py:28
  17.8 0.1 copy.20.mine_ref
  17.9 0.0 collective-permute-done.4
  17.9 2.7 %collective-permute-start.7 = (bf16[8,7168]{1,0:T(8,128)(2,1)S(1)}, bf16[8,7168]{1,0:T(8,128)(2,1)S(1)}, u32[]{:S(2)}, u32[]{:S(2)}) collective-permute-start(bf16[8,7168]{1,0:T(8,128)(2,1)S(1)} %dynamic-slice_bitcast_fusion), channel_id=1, source_target_pairs={{0,20},{4,24},{8,28},{12,0},{16,4},{20,8},{24,12},{28,16},{1,21},{... | collective-permute-start | bytes 344072 | tf_op jit(solution)/shard_map/ppermute | solution.py:28
  20.6 0.0 collective-permute-done.5
  20.6 1.3 %collective-permute-start.8 = (bf16[8,7168]{1,0:T(8,128)(2,1)S(1)}, bf16[8,7168]{1,0:T(8,128)(2,1)S(1)}, u32[]{:S(2)}, u32[]{:S(2)}) collective-permute-start(bf16[8,7168]{1,0:T(8,128)(2,1)S(1)} %dynamic-slice_bitcast_fusion), channel_id=1, source_target_pairs={{0,24},{4,28},{8,0},{12,4},{16,8},{20,12},{24,16},{28,20},{1,25},{... | collective-permute-start | bytes 344072 | tf_op jit(solution)/shard_map/ppermute | solution.py:28
  21.9 4.9 %collective-permute-done.6 = bf16[8,7168]{1,0:T(8,128)(2,1)S(1)} collective-permute-done((bf16[8,7168]{1,0:T(8,128)(2,1)S(1)}, bf16[8,7168]{1,0:T(8,128)(2,1)S(1)}, u32[]{:S(2)}, u32[]{:S(2)}) %collective-permute-start.6) | collective-permute-done | bytes 114720 | tf_op jit(solution)/shard_map/ppermute | solution.py:28
  26.8 4.5 %collective-permute-start.9 = (bf16[8,7168]{1,0:T(8,128)(2,1)S(1)}, bf16[8,7168]{1,0:T(8,128)(2,1)S(1)}, u32[]{:S(2)}, u32[]{:S(2)}) collective-permute-start(bf16[8,7168]{1,0:T(8,128)(2,1)S(1)} %dynamic-slice_bitcast_fusion), channel_id=1, source_target_pairs={{0,28},{4,0},{8,4},{12,8},{16,12},{20,16},{24,20},{28,24},{1,29},{... | collective-permute-start | bytes 344072 | tf_op jit(solution)/shard_map/ppermute | solution.py:28
  31.4 0.0 collective-permute-done.7
  31.4 0.0 copy-done.9
  31.4 0.1 collective-permute-start.11
  31.5 0.0 collective-permute-done.8
  31.5 0.5 collective-permute-start
  32.0 1.7 %collective-permute-done.9 = bf16[8,7168]{1,0:T(8,128)(2,1)S(1)} collective-permute-done((bf16[8,7168]{1,0:T(8,128)(2,1)S(1)}, bf16[8,7168]{1,0:T(8,128)(2,1)S(1)}, u32[]{:S(2)}, u32[]{:S(2)}) %collective-permute-start.9) | collective-permute-done | bytes 114720 | tf_op jit(solution)/shard_map/ppermute | solution.py:28
  33.7 0.0 copy-done.11
  33.7 0.1 convert_add_fusion
  33.9 1.2 %collective-permute-done = bf16[256,256]{0,1:T(8,128)(2,1)S(1)} collective-permute-done((bf16[256,256]{0,1:T(8,128)(2,1)S(1)}, bf16[256,256]{0,1:T(8,128)(2,1)S(1)}, u32[]{:S(2)}, u32[]{:S(2)}) %collective-permute-start) | collective-permute-done | bytes 131104 | tf_op jit(solution)/shard_map/ppermute | solution.py:241
  35.1 0.1 copy.21.taken_ref
  35.2 0.0 collective-permute-done.1.near_ref
  35.2 0.0 copy-start
  35.2 2.0 %copy-done = bf16[1,256,7168]{2,1,0:T(8,128)(2,1)S(1)} copy-done((bf16[1,256,7168]{2,1,0:T(8,128)(2,1)S(1)}, bf16[1,256,7168]{2,1,0:T(8,128)(2,1)}, u32[]{:S(2)}) %copy-start) | copy-done | bytes 3670040
  37.2 6.3 %shard_map.145 = (bf16[128,7168]{1,0:T(8,128)(2,1)S(1)}, bf16[128,7168]{1,0:T(8,128)(2,1)S(1)}) custom-call(bf16[256,256]{1,0:T(8,128)(2,1)S(1)} %copy.20.mine_ref, bf16[256,256]{1,0:T(8,128)(2,1)S(1)} %copy.21.taken_ref, bf16[256,7168]{1,0:T(8,128)(2,1)S(1)} %bitcast.32, bf16[256,7168]{1,0:T(8,128)(2,1)} %collective-permute-done.1.near_ref), custom_call_target="tpu_custom_call" | custom-call | tf_op jit(solution)/shard_map/pallas_call | solution.py:151
  43.5 0.0 copy-start.2
  43.5 1.2 %copy-done.2 = bf16[128,7168]{1,0:T(8,128)(2,1)} copy-done((bf16[128,7168]{1,0:T(8,128)(2,1)}, bf16[128,7168]{1,0:T(8,128)(2,1)S(1)}, u32[]{:S(2)}) %copy-start.2) | copy-done | bytes 1835032
  44.8 1.2 %copy-done.10 = bf16[128,7168]{1,0:T(8,128)(2,1)} copy-done((bf16[128,7168]{1,0:T(8,128)(2,1)}, bf16[128,7168]{1,0:T(8,128)(2,1)S(1)}, u32[]{:S(2)}) %copy-start.10) | copy-done | bytes 1835032
  46.0 5.2 %collective-permute-done.2.refs_4_ = bf16[128,7168]{1,0:T(8,128)(2,1)} collective-permute-done((bf16[128,7168]{1,0:T(8,128)(2,1)}, bf16[128,7168]{1,0:T(8,128)(2,1)}, u32[]{:S(2)}, u32[]{:S(2)}) %collective-permute-start.2) | collective-permute-done | bytes 1835040 | tf_op jit(solution)/shard_map/ppermute | solution.py:231
  51.3 0.0 collective-permute-start.12
  51.3 0.1 copy.28
  51.4 0.1 copy.29
  51.5 1.6 %collective-permute-start.10 = (bf16[128,7168]{1,0:T(8,128)(2,1)}, bf16[128,7168]{1,0:T(8,128)(2,1)}, u32[]{:S(2)}, u32[]{:S(2)}) collective-permute-start(bf16[128,7168]{1,0:T(8,128)(2,1)} %copy-done.10), channel_id=1, source_target_pairs={{0,2},{1,3},{2,0},{3,1},{4,6},{5,7},{6,4},{7,5},{8,10},{9,11},{10,... | collective-permute-start | bytes 5505032 | tf_op jit(solution)/shard_map/ppermute | solution.py:247
  53.1 0.0 copy-done.12
  53.1 0.0 copy-done.13
  53.1 0.0 copy-start.8
  53.2 0.8 bitcast_subtract_fusion
  54.0 0.0 collective-permute-done.11.refs_3_
  54.0 1.4 %collective-permute-done.12.refs_5_ = bf16[128,7168]{1,0:T(8,128)(2,1)} collective-permute-done((bf16[128,7168]{1,0:T(8,128)(2,1)}, bf16[128,7168]{1,0:T(8,128)(2,1)}, u32[]{:S(2)}, u32[]{:S(2)}) %collective-permute-start.12) | collective-permute-done | bytes 1835040 | tf_op jit(solution)/shard_map/ppermute | solution.py:249
  55.4 2.0 %copy-done.1 = bf16[1,256,7168]{2,1,0:T(8,128)(2,1)S(1)} copy-done((bf16[1,256,7168]{2,1,0:T(8,128)(2,1)S(1)}, bf16[1,256,7168]{2,1,0:T(8,128)(2,1)}, u32[]{:S(2)}) %copy-start.1) | copy-done | bytes 3670040
  57.4 8.9 %shard_map.146 = (bf16[256,7168]{1,0:T(8,128)(2,1)}, bf16[512,256]{1,0:T(8,128)(2,1)S(1)}) custom-call(bf16[256,512]{1,0:T(8,128)(2,1)S(1)} %maximum_bitcast_fusion.refs_0_, bf16[256,7168]{1,0:T(8,128)(2,1)S(1)} %bitcast.33, bf16[128,7168]{1,0:T(8,128)(2,1)S(1)} %bitcast.42, bf16[128,7168]{1,0:T(8,128)(2,1)} %collective-permute-done.11.refs_3_, ...), custom_call_target="tpu_custom_call" | custom-call | flops 3758096384 | bytes 15204352 | tf_op jit(solution)/shard_map/pallas_call | solution.py:188
  66.4 0.0 copy-done.4
  66.4 0.0 copy-done.6
  66.4 0.0 copy-done.8
  66.4 3.8 %shard_map.147 = (bf16[512,256]{1,0:T(8,128)(2,1)}, bf16[512,256]{1,0:T(8,128)(2,1)}, bf16[512,256]{1,0:T(8,128)(2,1)}) custom-call(bf16[512,256]{1,0:T(8,128)(2,1)S(1)} %bitcast.35, bf16[512,256]{1,0:T(8,128)(2,1)S(1)} %bitcast.37, bf16[512,256]{1,0:T(8,128)(2,1)S(1)} %bitcast.39, bf16[512,256]{1,0:T(8,128)(2,1)S(1)} %slice_dynamic-update-slice_fusion.g_ref), custom_call_target="tpu_custom_call" | custom-call | flops 671088640 | bytes 1835008 | tf_op jit(solution)/shard_map/pallas_call | solution.py:126
  70.2 24.1 %collective-permute-done.10.refs_1_ = bf16[128,7168]{1,0:T(8,128)(2,1)} collective-permute-done((bf16[128,7168]{1,0:T(8,128)(2,1)}, bf16[128,7168]{1,0:T(8,128)(2,1)}, u32[]{:S(2)}, u32[]{:S(2)}) %collective-permute-start.10) | collective-permute-done | bytes 1835040 | tf_op jit(solution)/shard_map/ppermute | solution.py:247
  94.3 5.6 %shard_map.148 = bf16[128,7168]{1,0:T(8,128)(2,1)} custom-call(bf16[128,7168]{1,0:T(8,128)(2,1)} %copy-done.2, bf16[128,7168]{1,0:T(8,128)(2,1)} %collective-permute-done.10.refs_1_), custom_call_target="tpu_custom_call" | custom-call | tf_op jit(solution)/shard_map/pallas_call | solution.py:212
  (15 shorter events, 0.2 us)
Async XLA Ops:
  0.6 33.1 %copy-start.11 = (bf16[1,2,8,7168]{3,2,1,0:T(8,128)(2,1)S(1)}, bf16[1,2,8,7168]{3,2,1,0:T(8,128)(2,1)}, u32[]{:S(2)}) copy-start(bf16[1,2,8,7168]{3,2,1,0:T(8,128)(2,1)} %param.14) | copy-start | bytes 688132
  0.6 34.5 %collective-permute-start.1 = (bf16[256,7168]{1,0:T(8,128)(2,1)}, bf16[256,7168]{1,0:T(8,128)(2,1)}, u32[]{:S(2)}, u32[]{:S(2)}) collective-permute-start(bf16[256,7168]{1,0:T(8,128)(2,1)} %bitcast.31), channel_id=1, source_target_pairs={{0,1},{1,0},{2,3},{3,2},{4,5},{5,4},{6,7},{7,6},{8,9},{9,8},{10,11... | collective-permute-start | bytes 11010056 | tf_op jit(solution)/shard_map/ppermute | solution.py:233
  2.7 13.7 %collective-permute-start.3 = (bf16[8,7168]{1,0:T(8,128)(2,1)S(1)}, bf16[8,7168]{1,0:T(8,128)(2,1)S(1)}, u32[]{:S(2)}, u32[]{:S(2)}) collective-permute-start(bf16[8,7168]{1,0:T(8,128)(2,1)S(1)} %dynamic-slice_bitcast_fusion), channel_id=1, source_target_pairs={{0,4},{4,8},{8,12},{12,16},{16,20},{20,24},{24,28},{28,0},{1,5},{5... | collective-permute-start | bytes 344072 | tf_op jit(solution)/shard_map/ppermute | solution.py:28
  5.3 12.6 %collective-permute-start.4 = (bf16[8,7168]{1,0:T(8,128)(2,1)S(1)}, bf16[8,7168]{1,0:T(8,128)(2,1)S(1)}, u32[]{:S(2)}, u32[]{:S(2)}) collective-permute-start(bf16[8,7168]{1,0:T(8,128)(2,1)S(1)} %dynamic-slice_bitcast_fusion), channel_id=1, source_target_pairs={{0,8},{4,12},{8,16},{12,20},{16,24},{20,28},{24,0},{28,4},{1,9},{5... | collective-permute-start | bytes 344072 | tf_op jit(solution)/shard_map/ppermute | solution.py:28
  6.8 13.7 %collective-permute-start.5 = (bf16[8,7168]{1,0:T(8,128)(2,1)S(1)}, bf16[8,7168]{1,0:T(8,128)(2,1)S(1)}, u32[]{:S(2)}, u32[]{:S(2)}) collective-permute-start(bf16[8,7168]{1,0:T(8,128)(2,1)S(1)} %dynamic-slice_bitcast_fusion), channel_id=1, source_target_pairs={{0,12},{4,16},{8,20},{12,24},{16,28},{20,0},{24,4},{28,8},{1,13},{... | collective-permute-start | bytes 344072 | tf_op jit(solution)/shard_map/ppermute | solution.py:28
  9.4 41.9 %collective-permute-start.2 = (bf16[128,7168]{1,0:T(8,128)(2,1)}, bf16[128,7168]{1,0:T(8,128)(2,1)}, u32[]{:S(2)}, u32[]{:S(2)}) collective-permute-start(bf16[128,7168]{1,0:T(8,128)(2,1)} %bitcast.40), channel_id=1, source_target_pairs={{0,2},{1,3},{2,0},{3,1},{4,6},{5,7},{6,4},{7,5},{8,10},{9,11},{10,... | collective-permute-start | bytes 5505032 | tf_op jit(solution)/shard_map/ppermute | solution.py:231
  10.9 0.9 copy-start.3
  11.9 0.9 copy-start.5
  12.8 0.9 copy-start.7
  13.8 17.6 %copy-start.9 = (bf16[1,128,7168]{2,1,0:T(8,128)(2,1)S(1)}, bf16[1,128,7168]{2,1,0:T(8,128)(2,1)}, u32[]{:S(2)}) copy-start(bf16[1,128,7168]{2,1,0:T(8,128)(2,1)} %param.13) | copy-start | bytes 5505028
  16.5 10.4 %collective-permute-start.6 = (bf16[8,7168]{1,0:T(8,128)(2,1)S(1)}, bf16[8,7168]{1,0:T(8,128)(2,1)S(1)}, u32[]{:S(2)}, u32[]{:S(2)}) collective-permute-start(bf16[8,7168]{1,0:T(8,128)(2,1)S(1)} %dynamic-slice_bitcast_fusion), channel_id=1, source_target_pairs={{0,16},{4,20},{8,24},{12,28},{16,0},{20,4},{24,8},{28,12},{1,17},{... | collective-permute-start | bytes 344072 | tf_op jit(solution)/shard_map/ppermute | solution.py:28
  17.9 13.5 %collective-permute-start.7 = (bf16[8,7168]{1,0:T(8,128)(2,1)S(1)}, bf16[8,7168]{1,0:T(8,128)(2,1)S(1)}, u32[]{:S(2)}, u32[]{:S(2)}) collective-permute-start(bf16[8,7168]{1,0:T(8,128)(2,1)S(1)} %dynamic-slice_bitcast_fusion), channel_id=1, source_target_pairs={{0,20},{4,24},{8,28},{12,0},{16,4},{20,8},{24,12},{28,16},{1,21},{... | collective-permute-start | bytes 344072 | tf_op jit(solution)/shard_map/ppermute | solution.py:28
  20.6 10.9 %collective-permute-start.8 = (bf16[8,7168]{1,0:T(8,128)(2,1)S(1)}, bf16[8,7168]{1,0:T(8,128)(2,1)S(1)}, u32[]{:S(2)}, u32[]{:S(2)}) collective-permute-start(bf16[8,7168]{1,0:T(8,128)(2,1)S(1)} %dynamic-slice_bitcast_fusion), channel_id=1, source_target_pairs={{0,24},{4,28},{8,0},{12,4},{16,8},{20,12},{24,16},{28,20},{1,25},{... | collective-permute-start | bytes 344072 | tf_op jit(solution)/shard_map/ppermute | solution.py:28
  26.8 6.9 %collective-permute-start.9 = (bf16[8,7168]{1,0:T(8,128)(2,1)S(1)}, bf16[8,7168]{1,0:T(8,128)(2,1)S(1)}, u32[]{:S(2)}, u32[]{:S(2)}) collective-permute-start(bf16[8,7168]{1,0:T(8,128)(2,1)S(1)} %dynamic-slice_bitcast_fusion), channel_id=1, source_target_pairs={{0,28},{4,0},{8,4},{12,8},{16,12},{20,16},{24,20},{28,24},{1,29},{... | collective-permute-start | bytes 344072 | tf_op jit(solution)/shard_map/ppermute | solution.py:28
  31.4 22.6 %collective-permute-start.11 = (bf16[128,7168]{1,0:T(8,128)(2,1)S(1)}, bf16[128,7168]{1,0:T(8,128)(2,1)}, u32[]{:S(2)}, u32[]{:S(2)}) collective-permute-start(bf16[128,7168]{1,0:T(8,128)(2,1)S(1)} %bitcast.41), channel_id=1, source_target_pairs={{0,1},{1,0},{2,3},{3,2},{4,5},{5,4},{6,7},{7,6},{8,9},{9,8},{10,11... | collective-permute-start | bytes 5505032 | tf_op jit(solution)/shard_map/ppermute | solution.py:232
  31.5 3.6 %collective-permute-start = (bf16[256,256]{0,1:T(8,128)(2,1)S(1)}, bf16[256,256]{0,1:T(8,128)(2,1)S(1)}, u32[]{:S(2)}, u32[]{:S(2)}) collective-permute-start(bf16[256,256]{0,1:T(8,128)(2,1)S(1)} %pad_maximum_fusion.1), channel_id=1, source_target_pairs={{0,1},{1,0},{2,3},{3,2},{4,5},{5,4},{6,7},{7,6},{8,9},{9,8},{10,11... | collective-permute-start | bytes 393224 | tf_op jit(solution)/shard_map/ppermute | solution.py:241
  35.2 2.0 %copy-start = (bf16[1,256,7168]{2,1,0:T(8,128)(2,1)S(1)}, bf16[1,256,7168]{2,1,0:T(8,128)(2,1)}, u32[]{:S(2)}) copy-start(bf16[1,256,7168]{2,1,0:T(8,128)(2,1)} %param.12) | copy-start | bytes 11010052
  37.2 15.9 %copy-start.12 = (f32[2,8,7168]{2,1,0:T(8,128)S(1)}, f32[2,8,7168]{2,1,0:T(8,128)}, u32[]{:S(2)}) copy-start(f32[2,8,7168]{2,1,0:T(8,128)} %param.15) | copy-start | bytes 1376260
  37.2 15.9 %copy-start.13 = (f32[2,8,7168]{2,1,0:T(8,128)S(1)}, f32[2,8,7168]{2,1,0:T(8,128)}, u32[]{:S(2)}) copy-start(f32[2,8,7168]{2,1,0:T(8,128)} %param.16) | copy-start | bytes 1376260
  43.5 1.3 %copy-start.2 = (bf16[128,7168]{1,0:T(8,128)(2,1)}, bf16[128,7168]{1,0:T(8,128)(2,1)S(1)}, u32[]{:S(2)}) copy-start(bf16[128,7168]{1,0:T(8,128)(2,1)S(1)} %get-tuple-element.25.refs_0_) | copy-start | bytes 5505028
  44.8 1.2 %copy-start.10 = (bf16[128,7168]{1,0:T(8,128)(2,1)}, bf16[128,7168]{1,0:T(8,128)(2,1)S(1)}, u32[]{:S(2)}) copy-start(bf16[128,7168]{1,0:T(8,128)(2,1)S(1)} %get-tuple-element.26) | copy-start | bytes 5505028
  51.3 4.1 %collective-permute-start.12 = (bf16[128,7168]{1,0:T(8,128)(2,1)}, bf16[128,7168]{1,0:T(8,128)(2,1)}, u32[]{:S(2)}, u32[]{:S(2)}) collective-permute-start(bf16[128,7168]{1,0:T(8,128)(2,1)} %collective-permute-done.2.refs_4_), channel_id=1, source_target_pairs={{0,1},{1,0},{2,3},{3,2},{4,5},{5,4},{6,7},{7,6},{8,9},{9,8},{10,11... | collective-permute-start | bytes 5505032 | tf_op jit(solution)/shard_map/ppermute | solution.py:249
  51.5 42.8 %collective-permute-start.10 = (bf16[128,7168]{1,0:T(8,128)(2,1)}, bf16[128,7168]{1,0:T(8,128)(2,1)}, u32[]{:S(2)}, u32[]{:S(2)}) collective-permute-start(bf16[128,7168]{1,0:T(8,128)(2,1)} %copy-done.10), channel_id=1, source_target_pairs={{0,2},{1,3},{2,0},{3,1},{4,6},{5,7},{6,4},{7,5},{8,10},{9,11},{10,... | collective-permute-start | bytes 5505032 | tf_op jit(solution)/shard_map/ppermute | solution.py:247
  53.1 13.3 %copy-start.4 = (bf16[1,512,256]{2,1,0:T(8,128)(2,1)S(1)}, bf16[1,512,256]{2,1,0:T(8,128)(2,1)}, u32[]{:S(2)}) copy-start(bf16[1,512,256]{2,1,0:T(8,128)(2,1)} %param.9) | copy-start | bytes 786436
  53.1 13.3 %copy-start.6 = (bf16[1,512,256]{2,1,0:T(8,128)(2,1)S(1)}, bf16[1,512,256]{2,1,0:T(8,128)(2,1)}, u32[]{:S(2)}) copy-start(bf16[1,512,256]{2,1,0:T(8,128)(2,1)} %param.10) | copy-start | bytes 786436
  53.1 13.3 %copy-start.8 = (bf16[1,512,256]{2,1,0:T(8,128)(2,1)S(1)}, bf16[1,512,256]{2,1,0:T(8,128)(2,1)}, u32[]{:S(2)}) copy-start(bf16[1,512,256]{2,1,0:T(8,128)(2,1)} %param.11) | copy-start | bytes 786436
  55.4 2.0 %copy-start.1 = (bf16[1,256,7168]{2,1,0:T(8,128)(2,1)S(1)}, bf16[1,256,7168]{2,1,0:T(8,128)(2,1)}, u32[]{:S(2)}) copy-start(bf16[1,256,7168]{2,1,0:T(8,128)(2,1)} %param.12) | copy-start | bytes 11010052

commit v3 on v2

--- a/solution.py
+++ b/solution.py
@@ -22,16 +22,17 @@
     return (new_global, new_momentum)
 
 
-def sum_replicas(local_sel):
+def swap_add(total, step):
     size = lax.axis_size("rep")
-    others = [
-        lax.ppermute(local_sel, "rep", [(r, (r + k) % size) for r in range(size)])
-        for k in range(1, size)
-    ]
-    total = local_sel.astype(jnp.float32)
-    for other in others:
-        total = total + other.astype(jnp.float32)
-    return total
+    other = lax.ppermute(total, "rep", [(r, r ^ step) for r in range(size)])
+    return total.astype(jnp.float32) + other.astype(jnp.float32)
+
+
+def sum_steps():
+    size = lax.axis_size("rep")
+    if size & (size - 1):
+        raise ValueError("rep")
+    return [1 << i for i in range(size.bit_length() - 1)]
 
 
 def outer_update(summed, global_params, momentum, frag_index):
@@ -199,26 +200,59 @@
 
 
 def add_kernel(*refs):
-    total = refs[0][...].astype(jnp.float32)
-    for part in refs[1:-1]:
-        total = total + part[...].astype(jnp.float32)
-    refs[-1][...] = total.astype(refs[-1].dtype)
+    count = (len(refs) - 4) // 2
+    parts, out = refs[:count], refs[count]
+    held, total, in_sems, out_sems = refs[count + 1 : 2 * count + 1], *refs[2 * count + 1 :]
+    rows, chunks = out.shape[0], out_sems.shape[0]
+    each = rows // chunks
+    reads = [
+        [
+            pltpu.make_async_copy(
+                part.at[pl.ds(c * each, each)], slot.at[pl.ds(c * each, each)], in_sems.at[c, i]
+            )
+            for i, (part, slot) in enumerate(zip(parts, held))
+        ]
+        for c in range(chunks)
+    ]
+    writes = [
+        pltpu.make_async_copy(
+            total.at[pl.ds(c * each, each)], out.at[pl.ds(c * each, each)], out_sems.at[c]
+        )
+        for c in range(chunks)
+    ]
+    for chunk in reads:
+        for read in chunk:
+            read.start()
+    for c in range(chunks):
+        for read in reads[c]:
+            read.wait()
+        here = slice(c * each, (c + 1) * each)
+        summed = held[0][here, :].astype(jnp.float32)
+        for slot in held[1:]:
+            summed = summed + slot[here, :].astype(jnp.float32)
+        total[here, :] = summed.astype(total.dtype)
+        writes[c].start()
+    for write in writes:
+        write.wait()
 
 
 def add_parts(parts):
     rows, cols = parts[0].shape
-    block = column_block(cols)
-    spec = pl.BlockSpec((rows, block), lambda i: (0, i))
+    chunks = max(1, min(4, rows // 16))
+    slot = pltpu.VMEM((rows, cols), jnp.bfloat16)
+    anywhere = pl.BlockSpec(memory_space=pl.ANY)
     return pl.pallas_call(
         add_kernel,
-        grid=(cols // block,),
-        in_specs=[spec] * len(parts),
-        out_specs=spec,
+        in_specs=[anywhere] * len(parts),
+        out_specs=anywhere,
         out_shape=jax.ShapeDtypeStruct((rows, cols), jnp.bfloat16),
+        scratch_shapes=[slot] * (len(parts) + 1)
+        + [pltpu.SemaphoreType.DMA((chunks, len(parts))), pltpu.SemaphoreType.DMA((chunks,))],
+        compiler_params=vmem(24),
     )(*parts)
 
 
-def inner_step(queries, keys, values, out_weight, cotangent, local_sel):
+def inner_step(queries, keys, values, out_weight, cotangent, local_sel, finish):
     weight_here = out_weight[0]
     cot_here = cotangent[0]
     own_rows = cot_here.shape[0]
@@ -233,7 +267,9 @@
     weight_near = lax.ppermute(weight_here, "tp", pairs)
 
     context = attention_forward(queries[0], keys[0], values[0])
-    summed = sum_replicas(local_sel)
+    summed = local_sel
+    for bit in sum_steps()[:1]:
+        summed = swap_add(summed, bit)
 
     give = jnp.concatenate(
         [rows_of(context, ((chip + k) % chips) * 2 + 1 - core, own_rows) for k in range(chips)]
@@ -255,24 +291,30 @@
         owners += [from_chip * 2 + core, from_chip * 2 + 1 - core]
     context_rows = jnp.concatenate([rows_of(context, o, own_rows) for o in owners])
     weight_grad, part_grad = projection_grads(context_rows.T, weight_here, blocks)
+    part_grad, summed = lax.optimization_barrier((part_grad, summed))
+    for bit in sum_steps()[1:]:
+        summed = swap_add(summed, bit)
     context_grad = jnp.zeros_like(context)
     for i, o in enumerate(owners):
         context_grad = lax.dynamic_update_slice_in_dim(
             context_grad, part_grad[i * own_rows : (i + 1) * own_rows], o * own_rows, 0
         )
     shaped = attention_backward(queries[0], keys[0], values[0], context_grad)
-    got, weight_grad, shaped = lax.optimization_barrier((got, weight_grad, shaped))
+    outer = finish(summed)
+    got, weight_grad, shaped, outer = lax.optimization_barrier((got, weight_grad, shaped, outer))
     branch_out = add_parts([own] + got)
-    return (branch_out[None], weight_grad[None], *[g[None] for g in shaped], summed)
+    return (branch_out[None], weight_grad[None], *[g[None] for g in shaped], *outer)
 
 
 def shards(
     queries, keys, values, out_weight, cotangent, local_params, global_params, momentum, frag_index
 ):
     local_sel = lax.dynamic_index_in_dim(local_params[0], frag_index[0], 0, keepdims=False)
-    *results, summed = inner_step(queries, keys, values, out_weight, cotangent, local_sel)
-    new_global, new_momentum = outer_update(summed, global_params, momentum, frag_index)
-    return (results[0], results[1], results[2], results[3], results[4], new_global, new_momentum)
+
+    def finish(summed):
+        return outer_update(summed, global_params, momentum, frag_index)
+
+    return inner_step(queries, keys, values, out_weight, cotangent, local_sel, finish)
 
 
 def solution(mesh):

time: 101 us -> 91.9 us (0.910)
  starting transfers between devices: 20.7 us -> 11.7 us
  waiting for transfers between devices: 38.7 us -> 41.8 us
  Pallas kernels: 26.7 us -> 24.6 us
    ppermute x1, waiting for transfers between devices: 24.1 us -> 5.07 us  [inner_step(): lax.ppermute(p, 'tp', chip_shift(size, k))]
    ppermute x1, waiting for transfers between devices: 5.24 us -> 19.4 us  [inner_step(): lax.ppermute(cot_here, 'tp', chip_shift(size, k))]
    ppermute x7 -> x3, starting transfers between devices: 16.5 us -> 6.19 us  [swap_add(): other = lax.ppermute(total, 'rep', [(r, r ^ step) for r in range(size)])]
    ppermute x7 -> x3, waiting for transfers between devices: 6.69 us -> 15.3 us  [swap_add(): other = lax.ppermute(total, 'rep', [(r, r ^ step) for r in range(size)])]
    pallas_call x1, Pallas kernels: 5.57 us -> 3.59 us  [add_parts(): pl.pallas_call(add_kernel, in_specs=[anywhere] * len(parts), out_specs=an...]
    ppermute x1, waiting for transfers between devices: 1.21 us -> 0.01 us  [inner_step(): taken = lax.ppermute(give, 'tp', pairs)]
    ppermute x1, starting transfers between devices: 1.52 us -> 2.6 us  [inner_step(): lax.ppermute(cot_here, 'tp', chip_shift(size, k))]
    unnamed x34 -> x32, local copies, waits for them, and re-layouts: 10.1 us -> 10.4 us
  transfers between devices with their start and end apart: 13 -> 9, of which waited for: 6 -> 6; matrix products, arithmetic and copies ran while one was open for 3% -> 2% of each run, Pallas kernels for 21% -> 23%
where the time goes in v3:
time: 91.9 us; the launch traced here: 91.3 us
  waiting for transfers between devices  41.8 us (45%)
  Pallas kernels  24.6 us (27%)
  starting transfers between devices  11.7 us (13%)
  local copies, waits for them, and re-layouts  10.7 us (12%)
  between operations  1.55 us (2%)
  other arithmetic  0.95 us (1%)
    ppermute x1, waiting for transfers between devices, inner_step(): lax.ppermute(cot_here, 'tp', chip_shift(size, k))  19.4 us
    ppermute x3, waiting for transfers between devices, swap_add(): other = lax.ppermute(total, 'rep', [(r, r ^ step) for r in range(size)])  15.3 us
    unnamed x32, local copies, waits for them, and re-layouts  10.4 us
    pallas_call x1, Pallas kernels, projection_grads(): pl.pallas_call(grads_kernel, grid=(cols // block,), in_specs=[pl.BlockSpe...  8.89 us
    pallas_call x1, Pallas kernels, branch_parts(): pl.pallas_call(branch_kernel, grid=(cols // block,), in_specs=[whole, who...  6.22 us
    ppermute x3, starting transfers between devices, swap_add(): other = lax.ppermute(total, 'rep', [(r, r ^ step) for r in range(size)])  6.19 us
    ppermute x1, waiting for transfers between devices, inner_step(): lax.ppermute(p, 'tp', chip_shift(size, k))  5.07 us
    pallas_call x1, Pallas kernels, attention_backward(): pl.pallas_call(backward_kernel, grid=(query.shape[1] // HD,), in_specs=[s...  3.81 us
  transfers between devices with their start and end apart: 9, of which 6 were waited for; matrix products, arithmetic and copies ran while one was open for 2% of the time, Pallas kernels for 23%

profile of v3, /device:TPU:0, one launch (start us, length us, event | category | flops | bytes accessed | tf_op | source)
XLA Modules:
  0.0 91.3 jit_solution(14022018352286083948)
XLA Ops:
  0.6 0.5 collective-permute-start.1
  1.1 2.6 %collective-permute-start.2 = (bf16[128,7168]{1,0:T(8,128)(2,1)}, bf16[128,7168]{1,0:T(8,128)(2,1)}, u32[]{:S(2)}, u32[]{:S(2)}) collective-permute-start(bf16[128,7168]{1,0:T(8,128)(2,1)} %bitcast.40), channel_id=1, source_target_pairs={{0,2},{1,3},{2,0},{3,1},{4,6},{5,7},{6,4},{7,5},{8,10},{9,11},{10,... | collective-permute-start | bytes 5505032 | tf_op jit(solution)/shard_map/ppermute | solution.py:265
  3.7 0.2 collective-permute-start.5
  3.9 0.0 copy-start.2
  3.9 0.9 %copy-done.2 = bf16[1,512,256]{2,1,0:T(8,128)(2,1)S(1)} copy-done((bf16[1,512,256]{2,1,0:T(8,128)(2,1)S(1)}, bf16[1,512,256]{2,1,0:T(8,128)(2,1)}, u32[]{:S(2)}) %copy-start.2) | copy-done | bytes 262168
  4.9 0.0 copy-start.4
  4.9 0.9 %copy-done.4 = bf16[1,512,256]{2,1,0:T(8,128)(2,1)S(1)} copy-done((bf16[1,512,256]{2,1,0:T(8,128)(2,1)S(1)}, bf16[1,512,256]{2,1,0:T(8,128)(2,1)}, u32[]{:S(2)}) %copy-start.4) | copy-done | bytes 262168
  5.8 0.0 copy-start.6
  5.8 0.9 %copy-done.6 = bf16[1,512,256]{2,1,0:T(8,128)(2,1)S(1)} copy-done((bf16[1,512,256]{2,1,0:T(8,128)(2,1)S(1)}, bf16[1,512,256]{2,1,0:T(8,128)(2,1)}, u32[]{:S(2)}) %copy-start.6) | copy-done | bytes 262168
  6.8 0.0 copy-start.10
  6.8 2.1 %shard_map.144 = bf16[512,256]{1,0:T(8,128)(2,1)S(1)} custom-call(bf16[512,256]{1,0:T(8,128)(2,1)S(1)} %bitcast.34, bf16[512,256]{1,0:T(8,128)(2,1)S(1)} %bitcast.36, bf16[512,256]{1,0:T(8,128)(2,1)S(1)} %bitcast.38), custom_call_target="tpu_custom_call" | custom-call | tf_op jit(solution)/shard_map/pallas_call | solution.py:115
  9.0 0.1 copy.26
  9.1 0.1 copy.27
  9.2 0.4 collective-permute-start
  10.3 0.0 copy-done.10
  10.3 1.6 %collective-permute-start.3 = (bf16[8,7168]{1,0:T(8,128)(2,1)S(1)}, bf16[8,7168]{1,0:T(8,128)(2,1)S(1)}, u32[]{:S(2)}, u32[]{:S(2)}) collective-permute-start(bf16[8,7168]{1,0:T(8,128)(2,1)S(1)} %dynamic-slice_bitcast_fusion), channel_id=1, source_target_pairs={{0,4},{4,0},{8,12},{12,8},{16,20},{20,16},{24,28},{28,24},{1,5},{5... | collective-permute-start | bytes 344072 | tf_op jit(solution)/shard_map/ppermute | solution.py:27
  11.9 0.1 copy.24
  12.0 0.1 copy.25
  12.2 0.1 copy.20.mine_ref
  12.3 3.4 %collective-permute-done.3 = bf16[8,7168]{1,0:T(8,128)(2,1)S(1)} collective-permute-done((bf16[8,7168]{1,0:T(8,128)(2,1)S(1)}, bf16[8,7168]{1,0:T(8,128)(2,1)S(1)}, u32[]{:S(2)}, u32[]{:S(2)}) %collective-permute-start.3) | collective-permute-done | bytes 114720 | tf_op jit(solution)/shard_map/ppermute | solution.py:27
  15.6 0.0 collective-permute-done
  15.7 0.1 copy.21.taken_ref
  15.8 0.0 collective-permute-done.1.near_ref
  15.8 0.0 copy-start
  15.8 2.0 %copy-done = bf16[1,256,7168]{2,1,0:T(8,128)(2,1)S(1)} copy-done((bf16[1,256,7168]{2,1,0:T(8,128)(2,1)S(1)}, bf16[1,256,7168]{2,1,0:T(8,128)(2,1)}, u32[]{:S(2)}) %copy-start) | copy-done | bytes 3670040
  17.8 6.2 %shard_map.145 = (bf16[128,7168]{1,0:T(8,128)(2,1)S(1)}, bf16[128,7168]{1,0:T(8,128)(2,1)S(1)}) custom-call(bf16[256,256]{1,0:T(8,128)(2,1)S(1)} %copy.20.mine_ref, bf16[256,256]{1,0:T(8,128)(2,1)S(1)} %copy.21.taken_ref, bf16[256,7168]{1,0:T(8,128)(2,1)S(1)} %bitcast.32, bf16[256,7168]{1,0:T(8,128)(2,1)} %collective-permute-done.1.near_ref), custom_call_target="tpu_custom_call" | custom-call | tf_op jit(solution)/shard_map/pallas_call | solution.py:152
  24.0 0.0 copy-start.9
  24.0 1.2 %copy-done.9 = bf16[128,7168]{1,0:T(8,128)(2,1)} copy-done((bf16[128,7168]{1,0:T(8,128)(2,1)}, bf16[128,7168]{1,0:T(8,128)(2,1)S(1)}, u32[]{:S(2)}) %copy-start.9) | copy-done | bytes 1835032
  25.3 19.4 %collective-permute-done.2.refs_4_ = bf16[128,7168]{1,0:T(8,128)(2,1)} collective-permute-done((bf16[128,7168]{1,0:T(8,128)(2,1)}, bf16[128,7168]{1,0:T(8,128)(2,1)}, u32[]{:S(2)}, u32[]{:S(2)}) %collective-permute-start.2) | collective-permute-done | bytes 1835040 | tf_op jit(solution)/shard_map/ppermute | solution.py:265
  44.7 0.0 collective-permute-start.6
  44.7 0.1 copy.28
  44.8 0.1 copy.29
  44.9 0.0 copy-start.3
  44.9 0.0 copy-start.5
  45.0 1.8 %collective-permute-start.4 = (bf16[128,7168]{1,0:T(8,128)(2,1)}, bf16[128,7168]{1,0:T(8,128)(2,1)S(1)}, u32[]{:S(2)}, u32[]{:S(2)}) collective-permute-start(bf16[128,7168]{1,0:T(8,128)(2,1)} %copy-done.9), channel_id=1, source_target_pairs={{0,2},{1,3},{2,0},{3,1},{4,6},{5,7},{6,4},{7,5},{8,10},{9,11},{10,... | collective-permute-start | bytes 5505032 | tf_op jit(solution)/shard_map/ppermute | solution.py:283
  46.8 0.0 collective-permute-done.5.refs_3_
  46.8 2.0 %collective-permute-done.6.refs_5_ = bf16[128,7168]{1,0:T(8,128)(2,1)} collective-permute-done((bf16[128,7168]{1,0:T(8,128)(2,1)}, bf16[128,7168]{1,0:T(8,128)(2,1)}, u32[]{:S(2)}, u32[]{:S(2)}) %collective-permute-start.6) | collective-permute-done | bytes 1835040 | tf_op jit(solution)/shard_map/ppermute | solution.py:285
  48.8 0.0 copy-start.1
  48.8 2.0 %copy-done.1 = bf16[1,256,7168]{2,1,0:T(8,128)(2,1)S(1)} copy-done((bf16[1,256,7168]{2,1,0:T(8,128)(2,1)S(1)}, bf16[1,256,7168]{2,1,0:T(8,128)(2,1)}, u32[]{:S(2)}) %copy-start.1) | copy-done | bytes 3670040
  50.8 0.0 copy-start.8
  50.8 1.5 %copy-done.8 = bf16[1,128,7168]{2,1,0:T(8,128)(2,1)S(1)} copy-done((bf16[1,128,7168]{2,1,0:T(8,128)(2,1)S(1)}, bf16[1,128,7168]{2,1,0:T(8,128)(2,1)}, u32[]{:S(2)}) %copy-start.8) | copy-done | bytes 1835032
  52.3 0.0 copy-start.7
  52.3 8.9 %shard_map.146 = (bf16[256,7168]{1,0:T(8,128)(2,1)}, bf16[512,256]{1,0:T(8,128)(2,1)S(1)}) custom-call(bf16[256,512]{1,0:T(8,128)(2,1)S(1)} %maximum_bitcast_fusion.refs_0_, bf16[256,7168]{1,0:T(8,128)(2,1)S(1)} %bitcast.33, bf16[128,7168]{1,0:T(8,128)(2,1)S(1)} %bitcast.42, bf16[128,7168]{1,0:T(8,128)(2,1)} %collective-permute-done.5.refs_3_, ...), custom_call_target="tpu_custom_call" | custom-call | flops 3758096384 | bytes 15204352 | tf_op jit(solution)/shard_map/pallas_call | solution.py:189
  61.2 1.8 %collective-permute-start.7 = (f32[8,7168]{1,0:T(8,128)S(1)}, f32[8,7168]{1,0:T(8,128)S(1)}, u32[]{:S(2)}, u32[]{:S(2)}) collective-permute-start(f32[8,7168]{1,0:T(8,128)S(1)} %convert_add_fusion), channel_id=1, source_target_pairs={{0,8},{4,12},{8,0},{12,4},{16,24},{20,28},{24,16},{28,20},{1,9},{5... | collective-permute-start | bytes 688136 | tf_op jit(solution)/shard_map/ppermute | solution.py:27
  63.1 0.0 copy-start.11
  63.1 0.0 copy-start.12
  63.1 5.8 %collective-permute-done.7 = f32[8,7168]{1,0:T(8,128)S(1)} collective-permute-done((f32[8,7168]{1,0:T(8,128)S(1)}, f32[8,7168]{1,0:T(8,128)S(1)}, u32[]{:S(2)}, u32[]{:S(2)}) %collective-permute-start.7) | collective-permute-done | bytes 229408 | tf_op jit(solution)/shard_map/ppermute | solution.py:27
  69.0 2.8 %collective-permute-start.8 = (f32[8,7168]{1,0:T(8,128)S(1)}, f32[8,7168]{1,0:T(8,128)S(1)}, u32[]{:S(2)}, u32[]{:S(2)}) collective-permute-start(f32[8,7168]{1,0:T(8,128)S(1)} %add.102), channel_id=1, source_target_pairs={{0,16},{4,20},{8,24},{12,28},{16,0},{20,4},{24,8},{28,12},{1,17},{... | collective-permute-start | bytes 688136 | tf_op jit(solution)/shard_map/ppermute | solution.py:27
  71.8 0.0 copy-done.3
  71.8 0.0 copy-done.5
  71.8 0.0 copy-done.7
  71.8 3.8 %shard_map.147 = (bf16[512,256]{1,0:T(8,128)(2,1)}, bf16[512,256]{1,0:T(8,128)(2,1)}, bf16[512,256]{1,0:T(8,128)(2,1)}) custom-call(bf16[512,256]{1,0:T(8,128)(2,1)S(1)} %bitcast.35, bf16[512,256]{1,0:T(8,128)(2,1)S(1)} %bitcast.37, bf16[512,256]{1,0:T(8,128)(2,1)S(1)} %bitcast.39, bf16[512,256]{1,0:T(8,128)(2,1)S(1)} %slice_dynamic-update-slice_fusion.g_ref), custom_call_target="tpu_custom_call" | custom-call | flops 671088640 | bytes 1835008 | tf_op jit(solution)/shard_map/pallas_call | solution.py:127
  75.6 6.1 %collective-permute-done.8 = f32[8,7168]{1,0:T(8,128)S(1)} collective-permute-done((f32[8,7168]{1,0:T(8,128)S(1)}, f32[8,7168]{1,0:T(8,128)S(1)}, u32[]{:S(2)}, u32[]{:S(2)}) %collective-permute-start.8) | collective-permute-done | bytes 229408 | tf_op jit(solution)/shard_map/ppermute | solution.py:27
  81.8 0.0 copy-done.11
  81.8 0.0 copy-done.12
  81.8 0.8 bitcast_add_fusion
  82.6 5.1 %collective-permute-done.4.refs_1_ = bf16[128,7168]{1,0:T(8,128)(2,1)S(1)} collective-permute-done((bf16[128,7168]{1,0:T(8,128)(2,1)}, bf16[128,7168]{1,0:T(8,128)(2,1)S(1)}, u32[]{:S(2)}, u32[]{:S(2)}) %collective-permute-start.4) | collective-permute-done | bytes 1835040 | tf_op jit(solution)/shard_map/ppermute | solution.py:283
  87.7 3.6 %shard_map.148 = bf16[128,7168]{1,0:T(8,128)(2,1)} custom-call(bf16[128,7168]{1,0:T(8,128)(2,1)S(1)} %get-tuple-element.29.refs_0_, bf16[128,7168]{1,0:T(8,128)(2,1)S(1)} %collective-permute-done.4.refs_1_), custom_call_target="tpu_custom_call" | custom-call | tf_op jit(solution)/shard_map/pallas_call | solution.py:244
  (12 shorter events, 0.2 us)
Async XLA Ops:
  0.6 15.1 %collective-permute-start.1 = (bf16[256,7168]{1,0:T(8,128)(2,1)}, bf16[256,7168]{1,0:T(8,128)(2,1)}, u32[]{:S(2)}, u32[]{:S(2)}) collective-permute-start(bf16[256,7168]{1,0:T(8,128)(2,1)} %bitcast.31), channel_id=1, source_target_pairs={{0,1},{1,0},{2,3},{3,2},{4,5},{5,4},{6,7},{7,6},{8,9},{9,8},{10,11... | collective-permute-start | bytes 11010056 | tf_op jit(solution)/shard_map/ppermute | solution.py:267
  1.1 43.5 %collective-permute-start.2 = (bf16[128,7168]{1,0:T(8,128)(2,1)}, bf16[128,7168]{1,0:T(8,128)(2,1)}, u32[]{:S(2)}, u32[]{:S(2)}) collective-permute-start(bf16[128,7168]{1,0:T(8,128)(2,1)} %bitcast.40), channel_id=1, source_target_pairs={{0,2},{1,3},{2,0},{3,1},{4,6},{5,7},{6,4},{7,5},{8,10},{9,11},{10,... | collective-permute-start | bytes 5505032 | tf_op jit(solution)/shard_map/ppermute | solution.py:265
  3.7 43.1 %collective-permute-start.5 = (bf16[128,7168]{1,0:T(8,128)(2,1)}, bf16[128,7168]{1,0:T(8,128)(2,1)}, u32[]{:S(2)}, u32[]{:S(2)}) collective-permute-start(bf16[128,7168]{1,0:T(8,128)(2,1)} %bitcast.41), channel_id=1, source_target_pairs={{0,1},{1,0},{2,3},{3,2},{4,5},{5,4},{6,7},{7,6},{8,9},{9,8},{10,11... | collective-permute-start | bytes 5505032 | tf_op jit(solution)/shard_map/ppermute | solution.py:266
  3.9 0.9 %copy-start.2 = (bf16[1,512,256]{2,1,0:T(8,128)(2,1)S(1)}, bf16[1,512,256]{2,1,0:T(8,128)(2,1)}, u32[]{:S(2)}) copy-start(bf16[1,512,256]{2,1,0:T(8,128)(2,1)} %param.9) | copy-start | bytes 786436
  4.9 0.9 %copy-start.4 = (bf16[1,512,256]{2,1,0:T(8,128)(2,1)S(1)}, bf16[1,512,256]{2,1,0:T(8,128)(2,1)}, u32[]{:S(2)}) copy-start(bf16[1,512,256]{2,1,0:T(8,128)(2,1)} %param.10) | copy-start | bytes 786436
  5.8 0.9 %copy-start.6 = (bf16[1,512,256]{2,1,0:T(8,128)(2,1)S(1)}, bf16[1,512,256]{2,1,0:T(8,128)(2,1)}, u32[]{:S(2)}) copy-start(bf16[1,512,256]{2,1,0:T(8,128)(2,1)} %param.11) | copy-start | bytes 786436
  6.8 3.5 %copy-start.10 = (bf16[1,2,8,7168]{3,2,1,0:T(8,128)(2,1)S(1)}, bf16[1,2,8,7168]{3,2,1,0:T(8,128)(2,1)}, u32[]{:S(2)}) copy-start(bf16[1,2,8,7168]{3,2,1,0:T(8,128)(2,1)} %param.14) | copy-start | bytes 688132
  9.2 6.4 %collective-permute-start = (bf16[256,256]{0,1:T(8,128)(2,1)S(1)}, bf16[256,256]{0,1:T(8,128)(2,1)S(1)}, u32[]{:S(2)}, u32[]{:S(2)}) collective-permute-start(bf16[256,256]{0,1:T(8,128)(2,1)S(1)} %pad_maximum_fusion.1), channel_id=1, source_target_pairs={{0,1},{1,0},{2,3},{3,2},{4,5},{5,4},{6,7},{7,6},{8,9},{9,8},{10,11... | collective-permute-start | bytes 393224 | tf_op jit(solution)/shard_map/ppermute | solution.py:277
  10.3 5.3 %collective-permute-start.3 = (bf16[8,7168]{1,0:T(8,128)(2,1)S(1)}, bf16[8,7168]{1,0:T(8,128)(2,1)S(1)}, u32[]{:S(2)}, u32[]{:S(2)}) collective-permute-start(bf16[8,7168]{1,0:T(8,128)(2,1)S(1)} %dynamic-slice_bitcast_fusion), channel_id=1, source_target_pairs={{0,4},{4,0},{8,12},{12,8},{16,20},{20,16},{24,28},{28,24},{1,5},{5... | collective-permute-start | bytes 344072 | tf_op jit(solution)/shard_map/ppermute | solution.py:27
  15.8 2.0 %copy-start = (bf16[1,256,7168]{2,1,0:T(8,128)(2,1)S(1)}, bf16[1,256,7168]{2,1,0:T(8,128)(2,1)}, u32[]{:S(2)}) copy-start(bf16[1,256,7168]{2,1,0:T(8,128)(2,1)} %param.12) | copy-start | bytes 11010052
  24.0 1.2 %copy-start.9 = (bf16[128,7168]{1,0:T(8,128)(2,1)}, bf16[128,7168]{1,0:T(8,128)(2,1)S(1)}, u32[]{:S(2)}) copy-start(bf16[128,7168]{1,0:T(8,128)(2,1)S(1)} %get-tuple-element.30) | copy-start | bytes 5505028
  44.7 4.1 %collective-permute-start.6 = (bf16[128,7168]{1,0:T(8,128)(2,1)}, bf16[128,7168]{1,0:T(8,128)(2,1)}, u32[]{:S(2)}, u32[]{:S(2)}) collective-permute-start(bf16[128,7168]{1,0:T(8,128)(2,1)} %collective-permute-done.2.refs_4_), channel_id=1, source_target_pairs={{0,1},{1,0},{2,3},{3,2},{4,5},{5,4},{6,7},{7,6},{8,9},{9,8},{10,11... | collective-permute-start | bytes 5505032 | tf_op jit(solution)/shard_map/ppermute | solution.py:285
  44.9 26.9 %copy-start.3 = (bf16[1,512,256]{2,1,0:T(8,128)(2,1)S(1)}, bf16[1,512,256]{2,1,0:T(8,128)(2,1)}, u32[]{:S(2)}) copy-start(bf16[1,512,256]{2,1,0:T(8,128)(2,1)} %param.9) | copy-start | bytes 786436
  44.9 26.9 %copy-start.5 = (bf16[1,512,256]{2,1,0:T(8,128)(2,1)S(1)}, bf16[1,512,256]{2,1,0:T(8,128)(2,1)}, u32[]{:S(2)}) copy-start(bf16[1,512,256]{2,1,0:T(8,128)(2,1)} %param.10) | copy-start | bytes 786436
  45.0 42.7 %collective-permute-start.4 = (bf16[128,7168]{1,0:T(8,128)(2,1)}, bf16[128,7168]{1,0:T(8,128)(2,1)S(1)}, u32[]{:S(2)}, u32[]{:S(2)}) collective-permute-start(bf16[128,7168]{1,0:T(8,128)(2,1)} %copy-done.9), channel_id=1, source_target_pairs={{0,2},{1,3},{2,0},{3,1},{4,6},{5,7},{6,4},{7,5},{8,10},{9,11},{10,... | collective-permute-start | bytes 5505032 | tf_op jit(solution)/shard_map/ppermute | solution.py:283
  48.8 2.0 %copy-start.1 = (bf16[1,256,7168]{2,1,0:T(8,128)(2,1)S(1)}, bf16[1,256,7168]{2,1,0:T(8,128)(2,1)}, u32[]{:S(2)}) copy-start(bf16[1,256,7168]{2,1,0:T(8,128)(2,1)} %param.12) | copy-start | bytes 11010052
  50.8 1.5 %copy-start.8 = (bf16[1,128,7168]{2,1,0:T(8,128)(2,1)S(1)}, bf16[1,128,7168]{2,1,0:T(8,128)(2,1)}, u32[]{:S(2)}) copy-start(bf16[1,128,7168]{2,1,0:T(8,128)(2,1)} %param.13) | copy-start | bytes 5505028
  52.3 19.5 %copy-start.7 = (bf16[1,512,256]{2,1,0:T(8,128)(2,1)S(1)}, bf16[1,512,256]{2,1,0:T(8,128)(2,1)}, u32[]{:S(2)}) copy-start(bf16[1,512,256]{2,1,0:T(8,128)(2,1)} %param.11) | copy-start | bytes 786436
  61.2 7.7 %collective-permute-start.7 = (f32[8,7168]{1,0:T(8,128)S(1)}, f32[8,7168]{1,0:T(8,128)S(1)}, u32[]{:S(2)}, u32[]{:S(2)}) collective-permute-start(f32[8,7168]{1,0:T(8,128)S(1)} %convert_add_fusion), channel_id=1, source_target_pairs={{0,8},{4,12},{8,0},{12,4},{16,24},{20,28},{24,16},{28,20},{1,9},{5... | collective-permute-start | bytes 688136 | tf_op jit(solution)/shard_map/ppermute | solution.py:27
  63.1 18.7 %copy-start.11 = (f32[2,8,7168]{2,1,0:T(8,128)S(1)}, f32[2,8,7168]{2,1,0:T(8,128)}, u32[]{:S(2)}) copy-start(f32[2,8,7168]{2,1,0:T(8,128)} %param.16) | copy-start | bytes 1376260
  63.1 18.7 %copy-start.12 = (f32[2,8,7168]{2,1,0:T(8,128)S(1)}, f32[2,8,7168]{2,1,0:T(8,128)}, u32[]{:S(2)}) copy-start(f32[2,8,7168]{2,1,0:T(8,128)} %param.15) | copy-start | bytes 1376260
  69.0 12.8 %collective-permute-start.8 = (f32[8,7168]{1,0:T(8,128)S(1)}, f32[8,7168]{1,0:T(8,128)S(1)}, u32[]{:S(2)}, u32[]{:S(2)}) collective-permute-start(f32[8,7168]{1,0:T(8,128)S(1)} %add.102), channel_id=1, source_target_pairs={{0,16},{4,20},{8,24},{12,28},{16,0},{20,4},{24,8},{28,12},{1,17},{... | collective-permute-start | bytes 688136 | tf_op jit(solution)/shard_map/ppermute | solution.py:27

commit v4 on v3

--- a/solution.py
+++ b/solution.py
@@ -1,3 +1,5 @@
+import functools
+
 import jax
 import jax.numpy as jnp
 from jax import lax
@@ -136,27 +138,38 @@
     )(query, key, value, grad)
 
 
+def row_pieces(rows):
+    half, quarter = rows // 2, rows // 4
+    if quarter % 16 == 0:
+        return [(0, quarter), (quarter, half), (half, rows)]
+    return [(0, half), (half, rows)]
+
+
 def branch_kernel(mine_ref, taken_ref, here_ref, near_ref, *out_refs):
     total = dot(mine_ref[...], here_ref[...], (1, 0)) + dot(taken_ref[...], near_ref[...], (1, 0))
-    rows = out_refs[0].shape[0]
-    for k, out in enumerate(out_refs):
-        out[...] = total[k * rows : (k + 1) * rows].astype(out.dtype)
+    first = 0
+    for out in out_refs:
+        rows = out.shape[0]
+        out[...] = total[first : first + rows].astype(out.dtype)
+        first += rows
 
 
 def branch_parts(mine, taken, here, near, chips):
     rows, cols = mine.shape[0] // chips, here.shape[1]
+    pieces = [end - first for first, end in row_pieces(rows)]
     block = column_block(cols)
     whole = pl.BlockSpec(mine.shape, lambda i: (0, 0))
     weight = pl.BlockSpec((here.shape[0], block), lambda i: (0, i))
-    out = jax.ShapeDtypeStruct((rows, cols), jnp.bfloat16)
-    return pl.pallas_call(
+    outs = pl.pallas_call(
         branch_kernel,
         grid=(cols // block,),
         in_specs=[whole, whole, weight, weight],
-        out_specs=[pl.BlockSpec((rows, block), lambda i: (0, i))] * chips,
-        out_shape=[out] * chips,
+        out_specs=[pl.BlockSpec((r, block), lambda i: (0, i)) for r in pieces] * chips,
+        out_shape=[jax.ShapeDtypeStruct((r, cols), jnp.bfloat16) for r in pieces] * chips,
         compiler_params=vmem(32),
     )(mine, taken, here, near)
+    count = len(pieces)
+    return [outs[k * count : (k + 1) * count] for k in range(chips)]
 
 
 def grads_kernel(*refs):
@@ -199,57 +212,64 @@
     )(context_t, weight, *cots)
 
 
-def add_kernel(*refs):
-    count = (len(refs) - 4) // 2
-    parts, out = refs[:count], refs[count]
-    held, total, in_sems, out_sems = refs[count + 1 : 2 * count + 1], *refs[2 * count + 1 :]
-    rows, chunks = out.shape[0], out_sems.shape[0]
-    each = rows // chunks
-    reads = [
-        [
-            pltpu.make_async_copy(
-                part.at[pl.ds(c * each, each)], slot.at[pl.ds(c * each, each)], in_sems.at[c, i]
-            )
-            for i, (part, slot) in enumerate(zip(parts, held))
-        ]
-        for c in range(chunks)
-    ]
-    writes = [
-        pltpu.make_async_copy(
-            total.at[pl.ds(c * each, each)], out.at[pl.ds(c * each, each)], out_sems.at[c]
-        )
-        for c in range(chunks)
-    ]
-    for chunk in reads:
-        for read in chunk:
+CHUNK = 16
+
+
+def add_kernel(groups, inputs, *refs):
+    arrays, out, scratch = refs[:inputs], refs[inputs], list(refs[inputs + 1 :])
+    in_sems, out_sems = scratch[-2:]
+    work, taken, done = [], 0, 0
+    for first, rows, count in groups:
+        parts, slots = arrays[taken : taken + count], scratch[taken : taken + count]
+        total = scratch[sum(g[2] for g in groups) + groups.index((first, rows, count))]
+        taken += count
+        for c in range(rows // CHUNK):
+            here = pl.ds(c * CHUNK, CHUNK)
+            reads = [
+                pltpu.make_async_copy(part.at[here], slot.at[here], in_sems.at[done, i])
+                for i, (part, slot) in enumerate(zip(parts, slots))
+            ]
+            there = pl.ds(first + c * CHUNK, CHUNK)
+            write = pltpu.make_async_copy(total.at[here], out.at[there], out_sems.at[done])
+            work.append((here, slots, total, reads, write))
+            done += 1
+    for _, _, _, reads, _ in work:
+        for read in reads:
             read.start()
-    for c in range(chunks):
-        for read in reads[c]:
+    for here, slots, total, reads, write in work:
+        for read in reads:
             read.wait()
-        here = slice(c * each, (c + 1) * each)
-        summed = held[0][here, :].astype(jnp.float32)
-        for slot in held[1:]:
+        summed = slots[0][here, :].astype(jnp.float32)
+        for slot in slots[1:]:
             summed = summed + slot[here, :].astype(jnp.float32)
         total[here, :] = summed.astype(total.dtype)
-        writes[c].start()
-    for write in writes:
+        write.start()
+    for _, _, _, _, write in work:
         write.wait()
 
 
-def add_parts(parts):
-    rows, cols = parts[0].shape
-    chunks = max(1, min(4, rows // 16))
-    slot = pltpu.VMEM((rows, cols), jnp.bfloat16)
+def add_parts(groups, rows, base=None):
+    cols = groups[0][1][0].shape[1]
+    arrays = [part for _, parts in groups for part in parts]
+    shapes = [(first, parts[0].shape[0], len(parts)) for first, parts in groups]
+    chunks = sum(r // CHUNK for _, r, _ in shapes)
+    slots = [pltpu.VMEM(a.shape, jnp.bfloat16) for a in arrays]
+    slots += [pltpu.VMEM((r, cols), jnp.bfloat16) for _, r, _ in shapes]
+    inputs = arrays if base is None else arrays + [base]
     anywhere = pl.BlockSpec(memory_space=pl.ANY)
     return pl.pallas_call(
-        add_kernel,
-        in_specs=[anywhere] * len(parts),
+        functools.partial(add_kernel, shapes, len(inputs)),
+        in_specs=[anywhere] * len(inputs),
         out_specs=anywhere,
         out_shape=jax.ShapeDtypeStruct((rows, cols), jnp.bfloat16),
-        scratch_shapes=[slot] * (len(parts) + 1)
-        + [pltpu.SemaphoreType.DMA((chunks, len(parts))), pltpu.SemaphoreType.DMA((chunks,))],
+        scratch_shapes=slots
+        + [
+            pltpu.SemaphoreType.DMA((chunks, max(n for _, _, n in shapes))),
+            pltpu.SemaphoreType.DMA((chunks,)),
+        ],
+        input_output_aliases={} if base is None else {len(arrays): 0},
         compiler_params=vmem(24),
-    )(*parts)
+    )(*inputs)
 
 
 def inner_step(queries, keys, values, out_weight, cotangent, local_sel, finish):
@@ -279,8 +299,12 @@
         [rows_of(context, ((chip + k) % chips) * 2 + core, own_rows) for k in range(chips)]
     )
     own, *far = branch_parts(mine, taken, weight_here, weight_near, chips)
-    far, cot_far, own, summed = lax.optimization_barrier((far, cot_far, own, summed))
-    got = [lax.ppermute(p, "tp", chip_shift(size, k)) for k, p in enumerate(far, 1)]
+    bounds = row_pieces(own_rows)
+    own, far, cot_far, summed = lax.optimization_barrier((own, far, cot_far, summed))
+    got = [
+        [lax.ppermute(p, "tp", chip_shift(size, k)) for p in pieces]
+        for k, pieces in enumerate(far, 1)
+    ]
 
     cot_far_near = [lax.ppermute(c, "tp", pairs) for c in cot_far]
     blocks = [cot_here, cot_near]
@@ -300,9 +324,16 @@
             context_grad, part_grad[i * own_rows : (i + 1) * own_rows], o * own_rows, 0
         )
     shaped = attention_backward(queries[0], keys[0], values[0], context_grad)
+    groups = [
+        (first, [own[i]] + [g[i] for g in got]) for i, (first, _) in enumerate(bounds)
+    ]
     outer = finish(summed)
-    got, weight_grad, shaped, outer = lax.optimization_barrier((got, weight_grad, shaped, outer))
-    branch_out = add_parts([own] + got)
+    first_groups, shaped = lax.optimization_barrier((groups[:-1], shaped))
+    early = add_parts([(bounds[i][0], g[1]) for i, g in enumerate(first_groups)], own_rows)
+    last, weight_grad, shaped, outer, early = lax.optimization_barrier(
+        (groups[-1][1], weight_grad, shaped, outer, early)
+    )
+    branch_out = add_parts([(bounds[-1][0], last)], own_rows, early)
     return (branch_out[None], weight_grad[None], *[g[None] for g in shaped], *outer)
 
 

time: 91.9 us -> 95.7 us (1.041)
  waiting for transfers between devices: 41.8 us -> 35.7 us
  Pallas kernels: 24.6 us -> 28 us
  local copies, waits for them, and re-layouts: 10.7 us -> 13.8 us
  other arithmetic: 0.95 us -> 2.61 us
  starting transfers between devices: 11.7 us -> 13.3 us
    ppermute x3, waiting for transfers between devices: 15.3 us -> 11 us  [swap_add(): other = lax.ppermute(total, 'rep', [(r, r ^ step) for r in range(size)])]
    pallas_call x1 -> x2, Pallas kernels: 3.59 us -> 6.84 us  [add_parts(): pl.pallas_call(functools.partial(add_kernel, shapes, len(inputs)), in_spe...]
    unnamed x32 -> x36, local copies, waits for them, and re-layouts: 10.4 us -> 12.9 us
    ppermute x1 -> x3, starting transfers between devices: 1.82 us -> 3.85 us  [inner_step(): lax.ppermute(p, 'tp', chip_shift(size, k))]
    ppermute x1, waiting for transfers between devices: 1.99 us -> 0.01 us  [inner_step(): cot_far_near = [lax.ppermute(c, 'tp', pairs) for c in cot_far]]
    ppermute x1 -> x3, waiting for transfers between devices: 5.07 us -> 6.21 us  [inner_step(): lax.ppermute(p, 'tp', chip_shift(size, k))]
    transpose x1, other arithmetic: 0.03 us -> 0.99 us  [inner_step(): weight_grad, part_grad = projection_grads(context_rows.T, weight_here, bl...]
  transfers between devices with their start and end apart: 9 -> 11, of which waited for: 6 -> 5; matrix products, arithmetic and copies ran while one was open for 2% -> 8% of each run, Pallas kernels for 23% -> 26%
where the time goes in v4:
time: 95.7 us; the launch traced here: 95 us
  waiting for transfers between devices  35.7 us (37%)
  Pallas kernels  28 us (29%)
  local copies, waits for them, and re-layouts  13.8 us (14%)
  starting transfers between devices  13.3 us (14%)
  other arithmetic  2.61 us (3%)
  between operations  1.52 us (2%)
    ppermute x1, waiting for transfers between devices, inner_step(): lax.ppermute(cot_here, 'tp', chip_shift(size, k))  18.5 us
    unnamed x36, local copies, waits for them, and re-layouts  12.9 us
    ppermute x3, waiting for transfers between devices, swap_add(): other = lax.ppermute(total, 'rep', [(r, r ^ step) for r in range(size)])  11 us
    pallas_call x1, Pallas kernels, projection_grads(): pl.pallas_call(grads_kernel, grid=(cols // block,), in_specs=[pl.BlockSpe...  8.9 us
    pallas_call x2, Pallas kernels, add_parts(): pl.pallas_call(functools.partial(add_kernel, shapes, len(inputs)), in_spe...  6.84 us
    pallas_call x1, Pallas kernels, branch_parts(): pl.pallas_call(branch_kernel, grid=(cols // block,), in_specs=[whole, who...  6.29 us
    ppermute x3, waiting for transfers between devices, inner_step(): lax.ppermute(p, 'tp', chip_shift(size, k))  6.21 us
    ppermute x3, starting transfers between devices, swap_add(): other = lax.ppermute(total, 'rep', [(r, r ^ step) for r in range(size)])  5.79 us
  transfers between devices with their start and end apart: 11, of which 5 were waited for; matrix products, arithmetic and copies ran while one was open for 8% of the time, Pallas kernels for 26%

profile of v4, /device:TPU:0, one launch (start us, length us, event | category | flops | bytes accessed | tf_op | source)
XLA Modules:
  0.0 95.0 jit_solution(11729366050864512375)
XLA Ops:
  0.6 0.5 collective-permute-start.1
  1.1 2.6 %collective-permute-start.2 = (bf16[128,7168]{1,0:T(8,128)(2,1)}, bf16[128,7168]{1,0:T(8,128)(2,1)}, u32[]{:S(2)}, u32[]{:S(2)}) collective-permute-start(bf16[128,7168]{1,0:T(8,128)(2,1)} %bitcast.40), channel_id=1, source_target_pairs={{0,2},{1,3},{2,0},{3,1},{4,6},{5,7},{6,4},{7,5},{8,10},{9,11},{10,... | collective-permute-start | bytes 5505032 | tf_op jit(solution)/shard_map/ppermute | solution.py:285
  3.7 0.2 collective-permute-start.5
  3.9 0.0 copy-start.2
  3.9 0.9 copy-done.2
  4.9 0.0 copy-start.4
  4.9 0.9 copy-done.4
  5.8 0.0 copy-start.6
  5.8 0.9 copy-done.6
  6.8 0.0 copy-start.12
  6.8 2.1 %shard_map.144 = bf16[512,256]{1,0:T(8,128)(2,1)S(1)} custom-call(bf16[512,256]{1,0:T(8,128)(2,1)S(1)} %bitcast.34, bf16[512,256]{1,0:T(8,128)(2,1)S(1)} %bitcast.36, bf16[512,256]{1,0:T(8,128)(2,1)S(1)} %bitcast.38), custom_call_target="tpu_custom_call" | custom-call | tf_op jit(solution)/shard_map/pallas_call | solution.py:117
  8.9 0.7 constant_dynamic-slice_fusion.1
  9.6 0.1 copy.27
  9.7 0.1 copy.28
  9.9 0.4 collective-permute-start
  10.9 0.0 copy-done.12
  11.0 1.6 %collective-permute-start.3 = (bf16[8,7168]{1,0:T(8,128)(2,1)S(1)}, bf16[8,7168]{1,0:T(8,128)(2,1)S(1)}, u32[]{:S(2)}, u32[]{:S(2)}) collective-permute-start(bf16[8,7168]{1,0:T(8,128)(2,1)S(1)} %dynamic-slice_bitcast_fusion), channel_id=1, source_target_pairs={{0,4},{4,0},{8,12},{12,8},{16,20},{20,16},{24,28},{28,24},{1,5},{5... | collective-permute-start | bytes 344072 | tf_op jit(solution)/shard_map/ppermute | solution.py:29
  12.5 0.1 copy.25
  12.7 0.1 copy.26
  12.8 0.0 copy-start.11
  12.8 0.1 copy.21.mine_ref
  12.9 3.3 %collective-permute-done.3 = bf16[8,7168]{1,0:T(8,128)(2,1)S(1)} collective-permute-done((bf16[8,7168]{1,0:T(8,128)(2,1)S(1)}, bf16[8,7168]{1,0:T(8,128)(2,1)S(1)}, u32[]{:S(2)}, u32[]{:S(2)}) %collective-permute-start.3) | collective-permute-done | bytes 114720 | tf_op jit(solution)/shard_map/ppermute | solution.py:29
  16.3 0.7 convert_add_fusion
  17.0 0.0 collective-permute-done
  17.0 0.1 copy.22.taken_ref
  17.1 0.0 copy-done.11
  17.1 0.0 collective-permute-done.1.near_ref
  17.1 0.0 copy-start
  17.1 2.0 %copy-done = bf16[1,256,7168]{2,1,0:T(8,128)(2,1)S(1)} copy-done((bf16[1,256,7168]{2,1,0:T(8,128)(2,1)S(1)}, bf16[1,256,7168]{2,1,0:T(8,128)(2,1)}, u32[]{:S(2)}) %copy-start) | copy-done | bytes 3670040
  19.1 6.3 %shard_map.145 = (bf16[32,7168]{1,0:T(8,128)(2,1)S(1)}, bf16[32,7168]{1,0:T(8,128)(2,1)S(1)}, bf16[64,7168]{1,0:T(8,128)(2,1)S(1)}, bf16[32,7168]{1,0:T(8,128)(2...) custom-call(bf16[256,256]{1,0:T(8,128)(2,1)S(1)} %copy.21.mine_ref, ...), custom_call_target="tpu_custom_call" | custom-call | tf_op jit(solution)/shard_map/pallas_call | solution.py:163
  25.4 0.0 copy-start.9
  25.4 0.8 copy-done.9
  26.2 18.5 %collective-permute-done.2.refs_4_ = bf16[128,7168]{1,0:T(8,128)(2,1)} collective-permute-done((bf16[128,7168]{1,0:T(8,128)(2,1)}, bf16[128,7168]{1,0:T(8,128)(2,1)}, u32[]{:S(2)}, u32[]{:S(2)}) %collective-permute-start.2) | collective-permute-done | bytes 1835040 | tf_op jit(solution)/shard_map/ppermute | solution.py:285
  44.7 0.0 collective-permute-start.6
  44.7 0.0 copy-start.7
  44.7 1.6 %copy.29 = bf16[128,256]{0,1:T(8,128)(2,1)} copy(bf16[128,256]{1,0:T(8,128)(2,1)} %get-tuple-element.83) | data formatting | bytes 131072
  46.3 1.6 %copy.30 = bf16[128,256]{0,1:T(8,128)(2,1)} copy(bf16[128,256]{1,0:T(8,128)(2,1)} %get-tuple-element.88) | data formatting | bytes 131072
  47.9 1.0 %maximum_bitcast_fusion.refs_0_ = bf16[256,512]{1,0:T(8,128)(2,1)S(1)} fusion(bf16[128,256]{0,1:T(8,128)(2,1)S(1)} %copy.28, bf16[128,256]{0,1:T(8,128)(2,1)} %copy-done.11, bf16[128,256]{0,1:T(8,128)(2,1)} %copy.30, bf16[128,256]{0,1:T(8,128)(2,1)} %copy.29), kind=kLoop, calls=%fused_computation | loop fusion | flops 1048576 | bytes 524288 | tf_op jit(solution)/shard_map/transpose | solution.py:317
  48.9 1.8 %collective-permute-start.7 = (bf16[32,7168]{1,0:T(8,128)(2,1)}, bf16[32,7168]{1,0:T(8,128)(2,1)S(1)}, u32[]{:S(2)}, u32[]{:S(2)}) collective-permute-start(bf16[32,7168]{1,0:T(8,128)(2,1)} %copy-done.9), channel_id=1, source_target_pairs={{0,2},{1,3},{2,0},{3,1},{4,6},{5,7},{6,4},{7,5},{8,10},{9,11},{10,... | collective-permute-start | bytes 1376264 | tf_op jit(solution)/shard_map/ppermute | solution.py:305
  50.7 0.3 collective-permute-start.8
  50.9 1.8 %collective-permute-start.4 = (bf16[64,7168]{1,0:T(8,128)(2,1)S(1)}, bf16[64,7168]{1,0:T(8,128)(2,1)S(1)}, u32[]{:S(2)}, u32[]{:S(2)}) collective-permute-start(bf16[64,7168]{1,0:T(8,128)(2,1)S(1)} %get-tuple-element.51), channel_id=1, source_target_pairs={{0,2},{1,3},{2,0},{3,1},{4,6},{5,7},{6,4},{7,5},{8,10},{9,11},{10,... | collective-permute-start | bytes 2752520 | tf_op jit(solution)/shard_map/ppermute | solution.py:305
  52.7 0.0 collective-permute-done.5.refs_3_
  52.7 0.0 collective-permute-done.6.refs_5_
  52.7 2.0 %copy-done.1 = bf16[1,256,7168]{2,1,0:T(8,128)(2,1)S(1)} copy-done((bf16[1,256,7168]{2,1,0:T(8,128)(2,1)S(1)}, bf16[1,256,7168]{2,1,0:T(8,128)(2,1)}, u32[]{:S(2)}) %copy-start.1) | copy-done | bytes 3670040
  54.8 1.5 %copy-done.8 = bf16[1,128,7168]{2,1,0:T(8,128)(2,1)S(1)} copy-done((bf16[1,128,7168]{2,1,0:T(8,128)(2,1)S(1)}, bf16[1,128,7168]{2,1,0:T(8,128)(2,1)}, u32[]{:S(2)}) %copy-start.8) | copy-done | bytes 1835032
  56.3 8.9 %shard_map.146 = (bf16[256,7168]{1,0:T(8,128)(2,1)}, bf16[512,256]{1,0:T(8,128)(2,1)S(1)}) custom-call(bf16[256,512]{1,0:T(8,128)(2,1)S(1)} %maximum_bitcast_fusion.refs_0_, bf16[256,7168]{1,0:T(8,128)(2,1)S(1)} %bitcast.33, bf16[128,7168]{1,0:T(8,128)(2,1)S(1)} %bitcast.42, bf16[128,7168]{1,0:T(8,128)(2,1)} %collective-permute-done.5.refs_3_, ...), custom_call_target="tpu_custom_call" | custom-call | flops 3758096384 | bytes 15204352 | tf_op jit(solution)/shard_map/pallas_call | solution.py:202
  65.2 0.0 copy-done.10
  65.2 1.6 %collective-permute-start.9 = (f32[8,7168]{1,0:T(8,128)S(1)}, f32[8,7168]{1,0:T(8,128)S(1)}, u32[]{:S(2)}, u32[]{:S(2)}) collective-permute-start(f32[8,7168]{1,0:T(8,128)S(1)} %copy-done.10), channel_id=1, source_target_pairs={{0,8},{4,12},{8,0},{12,4},{16,24},{20,28},{24,16},{28,20},{1,9},{5... | collective-permute-start | bytes 688136 | tf_op jit(solution)/shard_map/ppermute | solution.py:29
  66.8 5.5 %collective-permute-done.9 = f32[8,7168]{1,0:T(8,128)S(1)} collective-permute-done((f32[8,7168]{1,0:T(8,128)S(1)}, f32[8,7168]{1,0:T(8,128)S(1)}, u32[]{:S(2)}, u32[]{:S(2)}) %collective-permute-start.9) | collective-permute-done | bytes 229408 | tf_op jit(solution)/shard_map/ppermute | solution.py:29
  72.4 2.7 %collective-permute-start.10 = (f32[8,7168]{1,0:T(8,128)S(1)}, f32[8,7168]{1,0:T(8,128)S(1)}, u32[]{:S(2)}, u32[]{:S(2)}) collective-permute-start(f32[8,7168]{1,0:T(8,128)S(1)} %add.102), channel_id=1, source_target_pairs={{0,16},{4,20},{8,24},{12,28},{16,0},{20,4},{24,8},{28,12},{1,17},{... | collective-permute-start | bytes 688136 | tf_op jit(solution)/shard_map/ppermute | solution.py:29
  75.0 0.0 copy-done.7
  75.0 0.0 copy-done.3
  75.1 0.0 copy-done.5
  75.1 3.8 %shard_map.147 = (bf16[512,256]{1,0:T(8,128)(2,1)}, bf16[512,256]{1,0:T(8,128)(2,1)}, bf16[512,256]{1,0:T(8,128)(2,1)}) custom-call(bf16[512,256]{1,0:T(8,128)(2,1)S(1)} %bitcast.35, bf16[512,256]{1,0:T(8,128)(2,1)S(1)} %bitcast.37, bf16[512,256]{1,0:T(8,128)(2,1)S(1)} %bitcast.39, bf16[512,256]{1,0:T(8,128)(2,1)S(1)} %slice_dynamic-update-slice_fusion.g_ref), custom_call_target="tpu_custom_call" | custom-call | flops 671088640 | bytes 1835008 | tf_op jit(solution)/shard_map/pallas_call | solution.py:129
  78.9 0.0 collective-permute-done.7.refs_1_
  78.9 0.0 collective-permute-done.8.refs_3_
  78.9 0.0 copy-start.14
  78.9 3.4 %shard_map.148.refs_2_ = bf16[128,7168]{1,0:T(8,128)(2,1)} custom-call(bf16[32,7168]{1,0:T(8,128)(2,1)S(1)} %get-tuple-element.68.refs_0_, bf16[32,7168]{1,0:T(8,128)(2,1)S(1)} %collective-permute-done.7.refs_1_, bf16[32,7168]{1,0:T(8,128)(2,1)S(1)} %get-tuple-element.70.refs_2_, bf16[32,7168]{1,0:T(8,128)(2,1)S(1)} %collective-permute-done.8.refs_3_), custom_call_target="tpu_custom_call" | custom-call | tf_op jit(solution)/shard_map/pallas_call | solution.py:260
  82.3 2.2 %collective-permute-done.10 = f32[8,7168]{1,0:T(8,128)S(1)} collective-permute-done((f32[8,7168]{1,0:T(8,128)S(1)}, f32[8,7168]{1,0:T(8,128)S(1)}, u32[]{:S(2)}, u32[]{:S(2)}) %collective-permute-start.10) | collective-permute-done | bytes 229408 | tf_op jit(solution)/shard_map/ppermute | solution.py:29
  84.5 0.0 copy-done.13
  84.5 0.0 copy-done.14
  84.5 0.8 bitcast_add_fusion
  85.4 6.2 %collective-permute-done.4.refs_1_ = bf16[64,7168]{1,0:T(8,128)(2,1)S(1)} collective-permute-done((bf16[64,7168]{1,0:T(8,128)(2,1)S(1)}, bf16[64,7168]{1,0:T(8,128)(2,1)S(1)}, u32[]{:S(2)}, u32[]{:S(2)}) %collective-permute-start.4) | collective-permute-done | bytes 917536 | tf_op jit(solution)/shard_map/ppermute | solution.py:305
  91.6 3.4 %shard_map.149 = bf16[128,7168]{1,0:T(8,128)(2,1)} custom-call(bf16[64,7168]{1,0:T(8,128)(2,1)S(1)} %get-tuple-element.72.refs_0_, bf16[64,7168]{1,0:T(8,128)(2,1)S(1)} %collective-permute-done.4.refs_1_, bf16[128,7168]{1,0:T(8,128)(2,1)} %shard_map.148.refs_2_), custom_call_target="tpu_custom_call", output_to_operand_aliasing={{}: (2, {})} | custom-call | tf_op jit(solution)/shard_map/pallas_call | solution.py:260
  (15 shorter events, 0.2 us)
Async XLA Ops:
  0.6 16.5 %collective-permute-start.1 = (bf16[256,7168]{1,0:T(8,128)(2,1)}, bf16[256,7168]{1,0:T(8,128)(2,1)}, u32[]{:S(2)}, u32[]{:S(2)}) collective-permute-start(bf16[256,7168]{1,0:T(8,128)(2,1)} %bitcast.31), channel_id=1, source_target_pairs={{0,1},{1,0},{2,3},{3,2},{4,5},{5,4},{6,7},{7,6},{8,9},{9,8},{10,11... | collective-permute-start | bytes 11010056 | tf_op jit(solution)/shard_map/ppermute | solution.py:287
  1.1 43.5 %collective-permute-start.2 = (bf16[128,7168]{1,0:T(8,128)(2,1)}, bf16[128,7168]{1,0:T(8,128)(2,1)}, u32[]{:S(2)}, u32[]{:S(2)}) collective-permute-start(bf16[128,7168]{1,0:T(8,128)(2,1)} %bitcast.40), channel_id=1, source_target_pairs={{0,2},{1,3},{2,0},{3,1},{4,6},{5,7},{6,4},{7,5},{8,10},{9,11},{10,... | collective-permute-start | bytes 5505032 | tf_op jit(solution)/shard_map/ppermute | solution.py:285
  3.7 49.0 %collective-permute-start.5 = (bf16[128,7168]{1,0:T(8,128)(2,1)}, bf16[128,7168]{1,0:T(8,128)(2,1)}, u32[]{:S(2)}, u32[]{:S(2)}) collective-permute-start(bf16[128,7168]{1,0:T(8,128)(2,1)} %bitcast.41), channel_id=1, source_target_pairs={{0,1},{1,0},{2,3},{3,2},{4,5},{5,4},{6,7},{7,6},{8,9},{9,8},{10,11... | collective-permute-start | bytes 5505032 | tf_op jit(solution)/shard_map/ppermute | solution.py:286
  3.9 0.9 %copy-start.2 = (bf16[1,512,256]{2,1,0:T(8,128)(2,1)S(1)}, bf16[1,512,256]{2,1,0:T(8,128)(2,1)}, u32[]{:S(2)}) copy-start(bf16[1,512,256]{2,1,0:T(8,128)(2,1)} %param.9) | copy-start | bytes 786436
  4.9 0.9 %copy-start.4 = (bf16[1,512,256]{2,1,0:T(8,128)(2,1)S(1)}, bf16[1,512,256]{2,1,0:T(8,128)(2,1)}, u32[]{:S(2)}) copy-start(bf16[1,512,256]{2,1,0:T(8,128)(2,1)} %param.10) | copy-start | bytes 786436
  5.8 0.9 %copy-start.6 = (bf16[1,512,256]{2,1,0:T(8,128)(2,1)S(1)}, bf16[1,512,256]{2,1,0:T(8,128)(2,1)}, u32[]{:S(2)}) copy-start(bf16[1,512,256]{2,1,0:T(8,128)(2,1)} %param.11) | copy-start | bytes 786436
  6.8 4.2 %copy-start.12 = (bf16[1,2,8,7168]{3,2,1,0:T(8,128)(2,1)S(1)}, bf16[1,2,8,7168]{3,2,1,0:T(8,128)(2,1)}, u32[]{:S(2)}) copy-start(bf16[1,2,8,7168]{3,2,1,0:T(8,128)(2,1)} %param.14) | copy-start | bytes 688132
  9.9 7.1 %collective-permute-start = (bf16[256,256]{0,1:T(8,128)(2,1)S(1)}, bf16[256,256]{0,1:T(8,128)(2,1)S(1)}, u32[]{:S(2)}, u32[]{:S(2)}) collective-permute-start(bf16[256,256]{0,1:T(8,128)(2,1)S(1)} %pad_maximum_fusion.1), channel_id=1, source_target_pairs={{0,1},{1,0},{2,3},{3,2},{4,5},{5,4},{6,7},{7,6},{8,9},{9,8},{10,11... | collective-permute-start | bytes 393224 | tf_op jit(solution)/shard_map/ppermute | solution.py:297
  11.0 5.3 %collective-permute-start.3 = (bf16[8,7168]{1,0:T(8,128)(2,1)S(1)}, bf16[8,7168]{1,0:T(8,128)(2,1)S(1)}, u32[]{:S(2)}, u32[]{:S(2)}) collective-permute-start(bf16[8,7168]{1,0:T(8,128)(2,1)S(1)} %dynamic-slice_bitcast_fusion), channel_id=1, source_target_pairs={{0,4},{4,0},{8,12},{12,8},{16,20},{20,16},{24,28},{28,24},{1,5},{5... | collective-permute-start | bytes 344072 | tf_op jit(solution)/shard_map/ppermute | solution.py:29
  12.8 4.3 %copy-start.11 = (bf16[128,256]{0,1:T(8,128)(2,1)}, bf16[128,256]{0,1:T(8,128)(2,1)S(1)}, u32[]{:S(2)}) copy-start(bf16[128,256]{0,1:T(8,128)(2,1)S(1)} %copy.26) | copy-start | bytes 196612
  17.1 2.0 %copy-start = (bf16[1,256,7168]{2,1,0:T(8,128)(2,1)S(1)}, bf16[1,256,7168]{2,1,0:T(8,128)(2,1)}, u32[]{:S(2)}) copy-start(bf16[1,256,7168]{2,1,0:T(8,128)(2,1)} %param.12) | copy-start | bytes 11010052
  25.4 0.8 copy-start.9
  44.7 8.0 %collective-permute-start.6 = (bf16[128,7168]{1,0:T(8,128)(2,1)}, bf16[128,7168]{1,0:T(8,128)(2,1)}, u32[]{:S(2)}, u32[]{:S(2)}) collective-permute-start(bf16[128,7168]{1,0:T(8,128)(2,1)} %collective-permute-done.2.refs_4_), channel_id=1, source_target_pairs={{0,1},{1,0},{2,3},{3,2},{4,5},{5,4},{6,7},{7,6},{8,9},{9,8},{10,11... | collective-permute-start | bytes 5505032 | tf_op jit(solution)/shard_map/ppermute | solution.py:309
  44.7 30.4 %copy-start.7 = (bf16[1,512,256]{2,1,0:T(8,128)(2,1)S(1)}, bf16[1,512,256]{2,1,0:T(8,128)(2,1)}, u32[]{:S(2)}) copy-start(bf16[1,512,256]{2,1,0:T(8,128)(2,1)} %param.11) | copy-start | bytes 786436
  47.9 27.2 %copy-start.3 = (bf16[1,512,256]{2,1,0:T(8,128)(2,1)S(1)}, bf16[1,512,256]{2,1,0:T(8,128)(2,1)}, u32[]{:S(2)}) copy-start(bf16[1,512,256]{2,1,0:T(8,128)(2,1)} %param.9) | copy-start | bytes 786436
  47.9 27.2 %copy-start.5 = (bf16[1,512,256]{2,1,0:T(8,128)(2,1)S(1)}, bf16[1,512,256]{2,1,0:T(8,128)(2,1)}, u32[]{:S(2)}) copy-start(bf16[1,512,256]{2,1,0:T(8,128)(2,1)} %param.10) | copy-start | bytes 786436
  48.9 30.0 %collective-permute-start.7 = (bf16[32,7168]{1,0:T(8,128)(2,1)}, bf16[32,7168]{1,0:T(8,128)(2,1)S(1)}, u32[]{:S(2)}, u32[]{:S(2)}) collective-permute-start(bf16[32,7168]{1,0:T(8,128)(2,1)} %copy-done.9), channel_id=1, source_target_pairs={{0,2},{1,3},{2,0},{3,1},{4,6},{5,7},{6,4},{7,5},{8,10},{9,11},{10,... | collective-permute-start | bytes 1376264 | tf_op jit(solution)/shard_map/ppermute | solution.py:305
  50.7 28.2 %collective-permute-start.8 = (bf16[32,7168]{1,0:T(8,128)(2,1)S(1)}, bf16[32,7168]{1,0:T(8,128)(2,1)S(1)}, u32[]{:S(2)}, u32[]{:S(2)}) collective-permute-start(bf16[32,7168]{1,0:T(8,128)(2,1)S(1)} %get-tuple-element.57), channel_id=1, source_target_pairs={{0,2},{1,3},{2,0},{3,1},{4,6},{5,7},{6,4},{7,5},{8,10},{9,11},{10,... | collective-permute-start | bytes 1376264 | tf_op jit(solution)/shard_map/ppermute | solution.py:305
  50.9 40.6 %collective-permute-start.4 = (bf16[64,7168]{1,0:T(8,128)(2,1)S(1)}, bf16[64,7168]{1,0:T(8,128)(2,1)S(1)}, u32[]{:S(2)}, u32[]{:S(2)}) collective-permute-start(bf16[64,7168]{1,0:T(8,128)(2,1)S(1)} %get-tuple-element.51), channel_id=1, source_target_pairs={{0,2},{1,3},{2,0},{3,1},{4,6},{5,7},{6,4},{7,5},{8,10},{9,11},{10,... | collective-permute-start | bytes 2752520 | tf_op jit(solution)/shard_map/ppermute | solution.py:305
  52.7 2.0 %copy-start.1 = (bf16[1,256,7168]{2,1,0:T(8,128)(2,1)S(1)}, bf16[1,256,7168]{2,1,0:T(8,128)(2,1)}, u32[]{:S(2)}) copy-start(bf16[1,256,7168]{2,1,0:T(8,128)(2,1)} %param.12) | copy-start | bytes 11010052
  54.8 1.5 %copy-start.8 = (bf16[1,128,7168]{2,1,0:T(8,128)(2,1)S(1)}, bf16[1,128,7168]{2,1,0:T(8,128)(2,1)}, u32[]{:S(2)}) copy-start(bf16[1,128,7168]{2,1,0:T(8,128)(2,1)} %param.13) | copy-start | bytes 5505028
  56.3 8.9 %copy-start.10 = (f32[8,7168]{1,0:T(8,128)S(1)}, f32[8,7168]{1,0:T(8,128)}, u32[]{:S(2)}) copy-start(f32[8,7168]{1,0:T(8,128)} %convert_add_fusion) | copy-start | bytes 688132
  65.2 7.2 %collective-permute-start.9 = (f32[8,7168]{1,0:T(8,128)S(1)}, f32[8,7168]{1,0:T(8,128)S(1)}, u32[]{:S(2)}, u32[]{:S(2)}) collective-permute-start(f32[8,7168]{1,0:T(8,128)S(1)} %copy-done.10), channel_id=1, source_target_pairs={{0,8},{4,12},{8,0},{12,4},{16,24},{20,28},{24,16},{28,20},{1,9},{5... | collective-permute-start | bytes 688136 | tf_op jit(solution)/shard_map/ppermute | solution.py:29
  72.4 12.2 %collective-permute-start.10 = (f32[8,7168]{1,0:T(8,128)S(1)}, f32[8,7168]{1,0:T(8,128)S(1)}, u32[]{:S(2)}, u32[]{:S(2)}) collective-permute-start(f32[8,7168]{1,0:T(8,128)S(1)} %add.102), channel_id=1, source_target_pairs={{0,16},{4,20},{8,24},{12,28},{16,0},{20,4},{24,8},{28,12},{1,17},{... | collective-permute-start | bytes 688136 | tf_op jit(solution)/shard_map/ppermute | solution.py:29
  78.9 5.6 %copy-start.13 = (f32[2,8,7168]{2,1,0:T(8,128)S(1)}, f32[2,8,7168]{2,1,0:T(8,128)}, u32[]{:S(2)}) copy-start(f32[2,8,7168]{2,1,0:T(8,128)} %param.16) | copy-start | bytes 1376260
  78.9 5.6 %copy-start.14 = (f32[2,8,7168]{2,1,0:T(8,128)S(1)}, f32[2,8,7168]{2,1,0:T(8,128)}, u32[]{:S(2)}) copy-start(f32[2,8,7168]{2,1,0:T(8,128)} %param.15) | copy-start | bytes 1376260

commit v5 on v3

--- a/solution.py
+++ b/solution.py
@@ -197,59 +197,6 @@
         compiler_params=vmem(32),
         cost_estimate=cost(4 * tokens * features * cols, context_t, weight, *cots, *out),
     )(context_t, weight, *cots)
-
-
-def add_kernel(*refs):
-    count = (len(refs) - 4) // 2
-    parts, out = refs[:count], refs[count]
-    held, total, in_sems, out_sems = refs[count + 1 : 2 * count + 1], *refs[2 * count + 1 :]
-    rows, chunks = out.shape[0], out_sems.shape[0]
-    each = rows // chunks
-    reads = [
-        [
-            pltpu.make_async_copy(
-                part.at[pl.ds(c * each, each)], slot.at[pl.ds(c * each, each)], in_sems.at[c, i]
-            )
-            for i, (part, slot) in enumerate(zip(parts, held))
-        ]
-        for c in range(chunks)
-    ]
-    writes = [
-        pltpu.make_async_copy(
-            total.at[pl.ds(c * each, each)], out.at[pl.ds(c * each, each)], out_sems.at[c]
-        )
-        for c in range(chunks)
-    ]
-    for chunk in reads:
-        for read in chunk:
-            read.start()
-    for c in range(chunks):
-        for read in reads[c]:
-            read.wait()
-        here = slice(c * each, (c + 1) * each)
-        summed = held[0][here, :].astype(jnp.float32)
-        for slot in held[1:]:
-            summed = summed + slot[here, :].astype(jnp.float32)
-        total[here, :] = summed.astype(total.dtype)
-        writes[c].start()
-    for write in writes:
-        write.wait()
-
-
-def add_parts(parts):
-    rows, cols = parts[0].shape
-    chunks = max(1, min(4, rows // 16))
-    slot = pltpu.VMEM((rows, cols), jnp.bfloat16)
-    anywhere = pl.BlockSpec(memory_space=pl.ANY)
-    return pl.pallas_call(
-        add_kernel,
-        in_specs=[anywhere] * len(parts),
-        out_specs=anywhere,
-        out_shape=jax.ShapeDtypeStruct((rows, cols), jnp.bfloat16),
-        scratch_shapes=[slot] * (len(parts) + 1)
-        + [pltpu.SemaphoreType.DMA((chunks, len(parts))), pltpu.SemaphoreType.DMA((chunks,))],
-        compiler_params=vmem(24),
-    )(*parts)
 
 
 def inner_step(queries, keys, values, out_weight, cotangent, local_sel, finish):
@@ -302,7 +249,10 @@
     shaped = attention_backward(queries[0], keys[0], values[0], context_grad)
     outer = finish(summed)
     got, weight_grad, shaped, outer = lax.optimization_barrier((got, weight_grad, shaped, outer))
-    branch_out = add_parts([own] + got)
+    branch_out = own.astype(jnp.float32)
+    for part in got:
+        branch_out = branch_out + part.astype(jnp.float32)
+    branch_out = branch_out.astype(jnp.bfloat16)
     return (branch_out[None], weight_grad[None], *[g[None] for g in shaped], *outer)
 
 

time: 91.9 us -> 89.9 us (0.978)
  Pallas kernels: 24.6 us -> 21.1 us
  other arithmetic: 0.95 us -> 2.62 us
    pallas_call x1 -> x0, Pallas kernels: 3.59 us -> none  [add_parts(): pl.pallas_call(add_kernel, in_specs=[anywhere] * len(parts), out_specs=an...]
    broadcast_in_dim x0 -> x1, other arithmetic: none -> 1.66 us  [inner_step(): branch_out[None]]
  transfers between devices with their start and end apart: 9 -> 9, of which waited for: 6 -> 6; matrix products, arithmetic and copies ran while one was open for 2% -> 2% of each run, Pallas kernels for 23% -> 24%
where the time goes in v5:
time: 89.9 us; the launch traced here: 89.4 us
  waiting for transfers between devices  41.8 us (46%)
  Pallas kernels  21.1 us (23%)
  starting transfers between devices  11.7 us (13%)
  local copies, waits for them, and re-layouts  10.7 us (12%)
  other arithmetic  2.62 us (3%)
  between operations  1.55 us (2%)
    ppermute x1, waiting for transfers between devices, inner_step(): lax.ppermute(cot_here, 'tp', chip_shift(size, k))  19.4 us
    ppermute x3, waiting for transfers between devices, swap_add(): other = lax.ppermute(total, 'rep', [(r, r ^ step) for r in range(size)])  15.3 us
    unnamed x32, local copies, waits for them, and re-layouts  10.4 us
    pallas_call x1, Pallas kernels, projection_grads(): pl.pallas_call(grads_kernel, grid=(cols // block,), in_specs=[pl.BlockSpe...  8.89 us
    pallas_call x1, Pallas kernels, branch_parts(): pl.pallas_call(branch_kernel, grid=(cols // block,), in_specs=[whole, who...  6.22 us
    ppermute x3, starting transfers between devices, swap_add(): other = lax.ppermute(total, 'rep', [(r, r ^ step) for r in range(size)])  6.19 us
    ppermute x1, waiting for transfers between devices, inner_step(): lax.ppermute(p, 'tp', chip_shift(size, k))  5.07 us
    pallas_call x1, Pallas kernels, attention_backward(): pl.pallas_call(backward_kernel, grid=(query.shape[1] // HD,), in_specs=[s...  3.81 us
  transfers between devices with their start and end apart: 9, of which 6 were waited for; matrix products, arithmetic and copies ran while one was open for 2% of the time, Pallas kernels for 24%

profile of v5, /device:TPU:0, one launch (start us, length us, event | category | flops | bytes accessed | tf_op | source)
XLA Modules:
  0.0 89.4 jit_solution(10192031675187596712)
XLA Ops:
  0.6 0.5 collective-permute-start.1
  1.1 2.6 %collective-permute-start.2 = (bf16[128,7168]{1,0:T(8,128)(2,1)}, bf16[128,7168]{1,0:T(8,128)(2,1)}, u32[]{:S(2)}, u32[]{:S(2)}) collective-permute-start(bf16[128,7168]{1,0:T(8,128)(2,1)} %bitcast.41), channel_id=1, source_target_pairs={{0,2},{1,3},{2,0},{3,1},{4,6},{5,7},{6,4},{7,5},{8,10},{9,11},{10,... | collective-permute-start | bytes 5505032 | tf_op jit(solution)/shard_map/ppermute | solution.py:212
  3.7 0.2 collective-permute-start.5
  3.9 0.0 copy-start.2
  3.9 0.9 %copy-done.2 = bf16[1,512,256]{2,1,0:T(8,128)(2,1)S(1)} copy-done((bf16[1,512,256]{2,1,0:T(8,128)(2,1)S(1)}, bf16[1,512,256]{2,1,0:T(8,128)(2,1)}, u32[]{:S(2)}) %copy-start.2) | copy-done | bytes 262168
  4.9 0.0 copy-start.4
  4.9 0.9 %copy-done.4 = bf16[1,512,256]{2,1,0:T(8,128)(2,1)S(1)} copy-done((bf16[1,512,256]{2,1,0:T(8,128)(2,1)S(1)}, bf16[1,512,256]{2,1,0:T(8,128)(2,1)}, u32[]{:S(2)}) %copy-start.4) | copy-done | bytes 262168
  5.8 0.0 copy-start.6
  5.8 0.9 %copy-done.6 = bf16[1,512,256]{2,1,0:T(8,128)(2,1)S(1)} copy-done((bf16[1,512,256]{2,1,0:T(8,128)(2,1)S(1)}, bf16[1,512,256]{2,1,0:T(8,128)(2,1)}, u32[]{:S(2)}) %copy-start.6) | copy-done | bytes 262168
  6.8 0.0 copy-start.10
  6.8 2.1 %shard_map.144 = bf16[512,256]{1,0:T(8,128)(2,1)S(1)} custom-call(bf16[512,256]{1,0:T(8,128)(2,1)S(1)} %bitcast.35, bf16[512,256]{1,0:T(8,128)(2,1)S(1)} %bitcast.37, bf16[512,256]{1,0:T(8,128)(2,1)S(1)} %bitcast.39), custom_call_target="tpu_custom_call" | custom-call | tf_op jit(solution)/shard_map/pallas_call | solution.py:115
  9.0 0.1 copy.26
  9.1 0.1 copy.27
  9.2 0.4 collective-permute-start
  10.3 0.0 copy-done.10
  10.3 1.6 %collective-permute-start.3 = (bf16[8,7168]{1,0:T(8,128)(2,1)S(1)}, bf16[8,7168]{1,0:T(8,128)(2,1)S(1)}, u32[]{:S(2)}, u32[]{:S(2)}) collective-permute-start(bf16[8,7168]{1,0:T(8,128)(2,1)S(1)} %dynamic-slice_bitcast_fusion), channel_id=1, source_target_pairs={{0,4},{4,0},{8,12},{12,8},{16,20},{20,16},{24,28},{28,24},{1,5},{5... | collective-permute-start | bytes 344072 | tf_op jit(solution)/shard_map/ppermute | solution.py:27
  11.9 0.1 copy.24
  12.0 0.1 copy.25
  12.2 0.1 copy.20.mine_ref
  12.3 3.4 %collective-permute-done.3 = bf16[8,7168]{1,0:T(8,128)(2,1)S(1)} collective-permute-done((bf16[8,7168]{1,0:T(8,128)(2,1)S(1)}, bf16[8,7168]{1,0:T(8,128)(2,1)S(1)}, u32[]{:S(2)}, u32[]{:S(2)}) %collective-permute-start.3) | collective-permute-done | bytes 114720 | tf_op jit(solution)/shard_map/ppermute | solution.py:27
  15.6 0.0 collective-permute-done
  15.7 0.1 copy.21.taken_ref
  15.8 0.0 collective-permute-done.1.near_ref
  15.8 0.0 copy-start
  15.8 2.0 %copy-done = bf16[1,256,7168]{2,1,0:T(8,128)(2,1)S(1)} copy-done((bf16[1,256,7168]{2,1,0:T(8,128)(2,1)S(1)}, bf16[1,256,7168]{2,1,0:T(8,128)(2,1)}, u32[]{:S(2)}) %copy-start) | copy-done | bytes 3670040
  17.8 6.2 %shard_map.145 = (bf16[128,7168]{1,0:T(8,128)(2,1)S(1)}, bf16[128,7168]{1,0:T(8,128)(2,1)S(1)}) custom-call(bf16[256,256]{1,0:T(8,128)(2,1)S(1)} %copy.20.mine_ref, bf16[256,256]{1,0:T(8,128)(2,1)S(1)} %copy.21.taken_ref, bf16[256,7168]{1,0:T(8,128)(2,1)S(1)} %bitcast.33, bf16[256,7168]{1,0:T(8,128)(2,1)} %collective-permute-done.1.near_ref), custom_call_target="tpu_custom_call" | custom-call | tf_op jit(solution)/shard_map/pallas_call | solution.py:152
  24.0 0.0 copy-start.9
  24.0 1.2 %copy-done.9 = bf16[128,7168]{1,0:T(8,128)(2,1)} copy-done((bf16[128,7168]{1,0:T(8,128)(2,1)}, bf16[128,7168]{1,0:T(8,128)(2,1)S(1)}, u32[]{:S(2)}) %copy-start.9) | copy-done | bytes 1835032
  25.3 19.4 %collective-permute-done.2.refs_4_ = bf16[128,7168]{1,0:T(8,128)(2,1)} collective-permute-done((bf16[128,7168]{1,0:T(8,128)(2,1)}, bf16[128,7168]{1,0:T(8,128)(2,1)}, u32[]{:S(2)}, u32[]{:S(2)}) %collective-permute-start.2) | collective-permute-done | bytes 1835040 | tf_op jit(solution)/shard_map/ppermute | solution.py:212
  44.7 0.0 collective-permute-start.6
  44.7 0.1 copy.28
  44.8 0.1 copy.29
  44.9 0.0 copy-start.3
  44.9 0.0 copy-start.5
  45.0 1.8 %collective-permute-start.4 = (bf16[128,7168]{1,0:T(8,128)(2,1)}, bf16[128,7168]{1,0:T(8,128)(2,1)S(1)}, u32[]{:S(2)}, u32[]{:S(2)}) collective-permute-start(bf16[128,7168]{1,0:T(8,128)(2,1)} %copy-done.9), channel_id=1, source_target_pairs={{0,2},{1,3},{2,0},{3,1},{4,6},{5,7},{6,4},{7,5},{8,10},{9,11},{10,... | collective-permute-start | bytes 5505032 | tf_op jit(solution)/shard_map/ppermute | solution.py:230
  46.8 0.0 collective-permute-done.5.refs_3_
  46.8 2.0 %collective-permute-done.6.refs_5_ = bf16[128,7168]{1,0:T(8,128)(2,1)} collective-permute-done((bf16[128,7168]{1,0:T(8,128)(2,1)}, bf16[128,7168]{1,0:T(8,128)(2,1)}, u32[]{:S(2)}, u32[]{:S(2)}) %collective-permute-start.6) | collective-permute-done | bytes 1835040 | tf_op jit(solution)/shard_map/ppermute | solution.py:232
  48.8 0.0 copy-start.1
  48.8 2.0 %copy-done.1 = bf16[1,256,7168]{2,1,0:T(8,128)(2,1)S(1)} copy-done((bf16[1,256,7168]{2,1,0:T(8,128)(2,1)S(1)}, bf16[1,256,7168]{2,1,0:T(8,128)(2,1)}, u32[]{:S(2)}) %copy-start.1) | copy-done | bytes 3670040
  50.8 0.0 copy-start.8
  50.8 1.5 %copy-done.8 = bf16[1,128,7168]{2,1,0:T(8,128)(2,1)S(1)} copy-done((bf16[1,128,7168]{2,1,0:T(8,128)(2,1)S(1)}, bf16[1,128,7168]{2,1,0:T(8,128)(2,1)}, u32[]{:S(2)}) %copy-start.8) | copy-done | bytes 1835032
  52.3 0.0 copy-start.7
  52.3 8.9 %shard_map.146 = (bf16[256,7168]{1,0:T(8,128)(2,1)}, bf16[512,256]{1,0:T(8,128)(2,1)S(1)}) custom-call(bf16[256,512]{1,0:T(8,128)(2,1)S(1)} %maximum_bitcast_fusion.refs_0_, bf16[256,7168]{1,0:T(8,128)(2,1)S(1)} %bitcast.34, bf16[128,7168]{1,0:T(8,128)(2,1)S(1)} %bitcast.43, bf16[128,7168]{1,0:T(8,128)(2,1)} %collective-permute-done.5.refs_3_, ...), custom_call_target="tpu_custom_call" | custom-call | flops 3758096384 | bytes 15204352 | tf_op jit(solution)/shard_map/pallas_call | solution.py:189
  61.2 1.8 %collective-permute-start.7 = (f32[8,7168]{1,0:T(8,128)S(1)}, f32[8,7168]{1,0:T(8,128)S(1)}, u32[]{:S(2)}, u32[]{:S(2)}) collective-permute-start(f32[8,7168]{1,0:T(8,128)S(1)} %convert_add_fusion), channel_id=1, source_target_pairs={{0,8},{4,12},{8,0},{12,4},{16,24},{20,28},{24,16},{28,20},{1,9},{5... | collective-permute-start | bytes 688136 | tf_op jit(solution)/shard_map/ppermute | solution.py:27
  63.1 0.0 copy-start.11
  63.1 0.0 copy-start.12
  63.1 5.8 %collective-permute-done.7 = f32[8,7168]{1,0:T(8,128)S(1)} collective-permute-done((f32[8,7168]{1,0:T(8,128)S(1)}, f32[8,7168]{1,0:T(8,128)S(1)}, u32[]{:S(2)}, u32[]{:S(2)}) %collective-permute-start.7) | collective-permute-done | bytes 229408 | tf_op jit(solution)/shard_map/ppermute | solution.py:27
  69.0 2.8 %collective-permute-start.8 = (f32[8,7168]{1,0:T(8,128)S(1)}, f32[8,7168]{1,0:T(8,128)S(1)}, u32[]{:S(2)}, u32[]{:S(2)}) collective-permute-start(f32[8,7168]{1,0:T(8,128)S(1)} %add.105), channel_id=1, source_target_pairs={{0,16},{4,20},{8,24},{12,28},{16,0},{20,4},{24,8},{28,12},{1,17},{... | collective-permute-start | bytes 688136 | tf_op jit(solution)/shard_map/ppermute | solution.py:27
  71.8 0.0 copy-done.3
  71.8 0.0 copy-done.5
  71.8 0.0 copy-done.7
  71.8 3.8 %shard_map.147 = (bf16[512,256]{1,0:T(8,128)(2,1)}, bf16[512,256]{1,0:T(8,128)(2,1)}, bf16[512,256]{1,0:T(8,128)(2,1)}) custom-call(bf16[512,256]{1,0:T(8,128)(2,1)S(1)} %bitcast.36, bf16[512,256]{1,0:T(8,128)(2,1)S(1)} %bitcast.38, bf16[512,256]{1,0:T(8,128)(2,1)S(1)} %bitcast.40, bf16[512,256]{1,0:T(8,128)(2,1)S(1)} %slice_dynamic-update-slice_fusion.g_ref), custom_call_target="tpu_custom_call" | custom-call | flops 671088640 | bytes 1835008 | tf_op jit(solution)/shard_map/pallas_call | solution.py:127
  75.6 6.1 %collective-permute-done.8 = f32[8,7168]{1,0:T(8,128)S(1)} collective-permute-done((f32[8,7168]{1,0:T(8,128)S(1)}, f32[8,7168]{1,0:T(8,128)S(1)}, u32[]{:S(2)}, u32[]{:S(2)}) %collective-permute-start.8) | collective-permute-done | bytes 229408 | tf_op jit(solution)/shard_map/ppermute | solution.py:27
  81.8 0.0 copy-done.11
  81.8 0.0 copy-done.12
  81.8 0.8 bitcast_add_fusion
  82.6 5.1 %collective-permute-done.4 = bf16[128,7168]{1,0:T(8,128)(2,1)S(1)} collective-permute-done((bf16[128,7168]{1,0:T(8,128)(2,1)}, bf16[128,7168]{1,0:T(8,128)(2,1)S(1)}, u32[]{:S(2)}, u32[]{:S(2)}) %collective-permute-start.4) | collective-permute-done | bytes 1835040 | tf_op jit(solution)/shard_map/ppermute | solution.py:230
  87.7 1.7 %fusion = bf16[1,128,7168]{2,1,0:T(8,128)(2,1)} fusion(bf16[128,7168]{1,0:T(8,128)(2,1)S(1)} %collective-permute-done.4, bf16[128,7168]{1,0:T(8,128)(2,1)S(1)} %get-tuple-element.29), kind=kLoop, calls=%fused_computation.1 | loop fusion | flops 3670016 | bytes 5505024 | tf_op jit(solution)/shard_map/broadcast_in_dim | solution.py:256
  (12 shorter events, 0.2 us)
Async XLA Ops:
  0.6 15.1 %collective-permute-start.1 = (bf16[256,7168]{1,0:T(8,128)(2,1)}, bf16[256,7168]{1,0:T(8,128)(2,1)}, u32[]{:S(2)}, u32[]{:S(2)}) collective-permute-start(bf16[256,7168]{1,0:T(8,128)(2,1)} %bitcast.32), channel_id=1, source_target_pairs={{0,1},{1,0},{2,3},{3,2},{4,5},{5,4},{6,7},{7,6},{8,9},{9,8},{10,11... | collective-permute-start | bytes 11010056 | tf_op jit(solution)/shard_map/ppermute | solution.py:214
  1.1 43.5 %collective-permute-start.2 = (bf16[128,7168]{1,0:T(8,128)(2,1)}, bf16[128,7168]{1,0:T(8,128)(2,1)}, u32[]{:S(2)}, u32[]{:S(2)}) collective-permute-start(bf16[128,7168]{1,0:T(8,128)(2,1)} %bitcast.41), channel_id=1, source_target_pairs={{0,2},{1,3},{2,0},{3,1},{4,6},{5,7},{6,4},{7,5},{8,10},{9,11},{10,... | collective-permute-start | bytes 5505032 | tf_op jit(solution)/shard_map/ppermute | solution.py:212
  3.7 43.1 %collective-permute-start.5 = (bf16[128,7168]{1,0:T(8,128)(2,1)}, bf16[128,7168]{1,0:T(8,128)(2,1)}, u32[]{:S(2)}, u32[]{:S(2)}) collective-permute-start(bf16[128,7168]{1,0:T(8,128)(2,1)} %bitcast.42), channel_id=1, source_target_pairs={{0,1},{1,0},{2,3},{3,2},{4,5},{5,4},{6,7},{7,6},{8,9},{9,8},{10,11... | collective-permute-start | bytes 5505032 | tf_op jit(solution)/shard_map/ppermute | solution.py:213
  3.9 0.9 %copy-start.2 = (bf16[1,512,256]{2,1,0:T(8,128)(2,1)S(1)}, bf16[1,512,256]{2,1,0:T(8,128)(2,1)}, u32[]{:S(2)}) copy-start(bf16[1,512,256]{2,1,0:T(8,128)(2,1)} %param.9) | copy-start | bytes 786436
  4.9 0.9 %copy-start.4 = (bf16[1,512,256]{2,1,0:T(8,128)(2,1)S(1)}, bf16[1,512,256]{2,1,0:T(8,128)(2,1)}, u32[]{:S(2)}) copy-start(bf16[1,512,256]{2,1,0:T(8,128)(2,1)} %param.10) | copy-start | bytes 786436
  5.8 0.9 %copy-start.6 = (bf16[1,512,256]{2,1,0:T(8,128)(2,1)S(1)}, bf16[1,512,256]{2,1,0:T(8,128)(2,1)}, u32[]{:S(2)}) copy-start(bf16[1,512,256]{2,1,0:T(8,128)(2,1)} %param.11) | copy-start | bytes 786436
  6.8 3.5 %copy-start.10 = (bf16[1,2,8,7168]{3,2,1,0:T(8,128)(2,1)S(1)}, bf16[1,2,8,7168]{3,2,1,0:T(8,128)(2,1)}, u32[]{:S(2)}) copy-start(bf16[1,2,8,7168]{3,2,1,0:T(8,128)(2,1)} %param.14) | copy-start | bytes 688132
  9.2 6.4 %collective-permute-start = (bf16[256,256]{0,1:T(8,128)(2,1)S(1)}, bf16[256,256]{0,1:T(8,128)(2,1)S(1)}, u32[]{:S(2)}, u32[]{:S(2)}) collective-permute-start(bf16[256,256]{0,1:T(8,128)(2,1)S(1)} %pad_maximum_fusion.1), channel_id=1, source_target_pairs={{0,1},{1,0},{2,3},{3,2},{4,5},{5,4},{6,7},{7,6},{8,9},{9,8},{10,11... | collective-permute-start | bytes 393224 | tf_op jit(solution)/shard_map/ppermute | solution.py:224
  10.3 5.3 %collective-permute-start.3 = (bf16[8,7168]{1,0:T(8,128)(2,1)S(1)}, bf16[8,7168]{1,0:T(8,128)(2,1)S(1)}, u32[]{:S(2)}, u32[]{:S(2)}) collective-permute-start(bf16[8,7168]{1,0:T(8,128)(2,1)S(1)} %dynamic-slice_bitcast_fusion), channel_id=1, source_target_pairs={{0,4},{4,0},{8,12},{12,8},{16,20},{20,16},{24,28},{28,24},{1,5},{5... | collective-permute-start | bytes 344072 | tf_op jit(solution)/shard_map/ppermute | solution.py:27
  15.8 2.0 %copy-start = (bf16[1,256,7168]{2,1,0:T(8,128)(2,1)S(1)}, bf16[1,256,7168]{2,1,0:T(8,128)(2,1)}, u32[]{:S(2)}) copy-start(bf16[1,256,7168]{2,1,0:T(8,128)(2,1)} %param.12) | copy-start | bytes 11010052
  24.0 1.2 %copy-start.9 = (bf16[128,7168]{1,0:T(8,128)(2,1)}, bf16[128,7168]{1,0:T(8,128)(2,1)S(1)}, u32[]{:S(2)}) copy-start(bf16[128,7168]{1,0:T(8,128)(2,1)S(1)} %get-tuple-element.30) | copy-start | bytes 5505028
  44.7 4.1 %collective-permute-start.6 = (bf16[128,7168]{1,0:T(8,128)(2,1)}, bf16[128,7168]{1,0:T(8,128)(2,1)}, u32[]{:S(2)}, u32[]{:S(2)}) collective-permute-start(bf16[128,7168]{1,0:T(8,128)(2,1)} %collective-permute-done.2.refs_4_), channel_id=1, source_target_pairs={{0,1},{1,0},{2,3},{3,2},{4,5},{5,4},{6,7},{7,6},{8,9},{9,8},{10,11... | collective-permute-start | bytes 5505032 | tf_op jit(solution)/shard_map/ppermute | solution.py:232
  44.9 26.9 %copy-start.3 = (bf16[1,512,256]{2,1,0:T(8,128)(2,1)S(1)}, bf16[1,512,256]{2,1,0:T(8,128)(2,1)}, u32[]{:S(2)}) copy-start(bf16[1,512,256]{2,1,0:T(8,128)(2,1)} %param.9) | copy-start | bytes 786436
  44.9 26.9 %copy-start.5 = (bf16[1,512,256]{2,1,0:T(8,128)(2,1)S(1)}, bf16[1,512,256]{2,1,0:T(8,128)(2,1)}, u32[]{:S(2)}) copy-start(bf16[1,512,256]{2,1,0:T(8,128)(2,1)} %param.10) | copy-start | bytes 786436
  45.0 42.7 %collective-permute-start.4 = (bf16[128,7168]{1,0:T(8,128)(2,1)}, bf16[128,7168]{1,0:T(8,128)(2,1)S(1)}, u32[]{:S(2)}, u32[]{:S(2)}) collective-permute-start(bf16[128,7168]{1,0:T(8,128)(2,1)} %copy-done.9), channel_id=1, source_target_pairs={{0,2},{1,3},{2,0},{3,1},{4,6},{5,7},{6,4},{7,5},{8,10},{9,11},{10,... | collective-permute-start | bytes 5505032 | tf_op jit(solution)/shard_map/ppermute | solution.py:230
  48.8 2.0 %copy-start.1 = (bf16[1,256,7168]{2,1,0:T(8,128)(2,1)S(1)}, bf16[1,256,7168]{2,1,0:T(8,128)(2,1)}, u32[]{:S(2)}) copy-start(bf16[1,256,7168]{2,1,0:T(8,128)(2,1)} %param.12) | copy-start | bytes 11010052
  50.8 1.5 %copy-start.8 = (bf16[1,128,7168]{2,1,0:T(8,128)(2,1)S(1)}, bf16[1,128,7168]{2,1,0:T(8,128)(2,1)}, u32[]{:S(2)}) copy-start(bf16[1,128,7168]{2,1,0:T(8,128)(2,1)} %param.13) | copy-start | bytes 5505028
  52.3 19.5 %copy-start.7 = (bf16[1,512,256]{2,1,0:T(8,128)(2,1)S(1)}, bf16[1,512,256]{2,1,0:T(8,128)(2,1)}, u32[]{:S(2)}) copy-start(bf16[1,512,256]{2,1,0:T(8,128)(2,1)} %param.11) | copy-start | bytes 786436
  61.2 7.7 %collective-permute-start.7 = (f32[8,7168]{1,0:T(8,128)S(1)}, f32[8,7168]{1,0:T(8,128)S(1)}, u32[]{:S(2)}, u32[]{:S(2)}) collective-permute-start(f32[8,7168]{1,0:T(8,128)S(1)} %convert_add_fusion), channel_id=1, source_target_pairs={{0,8},{4,12},{8,0},{12,4},{16,24},{20,28},{24,16},{28,20},{1,9},{5... | collective-permute-start | bytes 688136 | tf_op jit(solution)/shard_map/ppermute | solution.py:27
  63.1 18.7 %copy-start.11 = (f32[2,8,7168]{2,1,0:T(8,128)S(1)}, f32[2,8,7168]{2,1,0:T(8,128)}, u32[]{:S(2)}) copy-start(f32[2,8,7168]{2,1,0:T(8,128)} %param.16) | copy-start | bytes 1376260
  63.1 18.7 %copy-start.12 = (f32[2,8,7168]{2,1,0:T(8,128)S(1)}, f32[2,8,7168]{2,1,0:T(8,128)}, u32[]{:S(2)}) copy-start(f32[2,8,7168]{2,1,0:T(8,128)} %param.15) | copy-start | bytes 1376260
  69.0 12.8 %collective-permute-start.8 = (f32[8,7168]{1,0:T(8,128)S(1)}, f32[8,7168]{1,0:T(8,128)S(1)}, u32[]{:S(2)}, u32[]{:S(2)}) collective-permute-start(f32[8,7168]{1,0:T(8,128)S(1)} %add.105), channel_id=1, source_target_pairs={{0,16},{4,20},{8,24},{12,28},{16,0},{20,4},{24,8},{28,12},{1,17},{... | collective-permute-start | bytes 688136 | tf_op jit(solution)/shard_map/ppermute | solution.py:27
